TPU v7x, 512 devices: a whole 4x8x8 slice. The times are simulated.
512 devices in a mesh: blk: 32 (over y, x), gz: 16 (over z, core).
Axes of the slice: x: 4, y: 8, z: 8, core: 2. Of those that a mesh axis runs over, the one named last changes fastest.
Arguments:
- velocity: bfloat16 [3, 32, 128, 16, 2048], P(None, None, 'blk', None, 'gz'), may hold values from -6 to 6
- metric: float32 [3, 128, 16, 2048], P(None, 'blk', None, 'gz'), may hold values from 0.5 to 2
- face_flip: int32 [32], P('blk'), may hold values from 0 to 1
Outputs:
- spatial_modes: float32 [4, 16, 128, 16, 2048], P(None, None, 'blk', None, 'gz')
- r_factor: float32 [32, 32], replicated
Inputs may be any that keep to these rules, and one draw needn't show every extreme that they name: `face_flip`: 1 marks a brick whose lower x face meets the brick before it mirrored in y; the first brick's entry is not read.
All inputs are finite; a program needn't handle non-finite values.
Results may differ from a plain program's by a relative error of at most 0.0003.
Values may be sent and summed in bfloat16 or wider, within the bound.
No kernel may reach another device: no remote copies, remote signals or barrier semaphores. Data moves between devices by JAX's collectives and lax.ppermute only.
A program may use at most 64 MiB of HBM per device.

v0:
```python
import jax
import jax.numpy as jnp
from jax import lax
from jax.sharding import PartitionSpec as P

KEEP = 16


def passed_along(value, axis, by):
    peers = lax.axis_size(axis)
    pairs = [(i, i + by) for i in range(peers) if 0 <= i + by < peers]
    return lax.ppermute(value, axis, pairs)


def padded(block, sides, width):
    for axis, dim in sides:
        count = lax.axis_size(axis)
        forward = [(i, i + 1) for i in range(count - 1)]
        forward.append((count - 1, 0))
        backward = [(target, source) for source, target in forward]
        low = lax.ppermute(
            lax.slice_in_dim(block, block.shape[dim] - width, None, axis=dim), axis, forward
        )
        high = lax.ppermute(lax.slice_in_dim(block, 0, width, axis=dim), axis, backward)
        block = jnp.concatenate([low, block, high], axis=dim)
    return block


def upper_factor(gram):
    order = gram.shape[0]
    rows = jnp.arange(order, dtype=jnp.int32)
    factor = jnp.zeros((order, order), jnp.float32)
    for column in range(order):
        partial_value = gram[column] - jnp.dot(
            factor[:, column], factor, precision=lax.Precision.HIGHEST
        )
        pivot = jnp.sqrt(partial_value[column])
        new_row = jnp.where(rows >= column, partial_value / pivot, 0.0)
        factor = factor + jnp.where((rows == column)[:, None], new_row[None, :], 0.0)
    return factor


def upper_inverse(factor):
    order = factor.shape[0]
    rows = jnp.arange(order, dtype=jnp.int32)
    inverse = jnp.zeros((order, order), jnp.float32)
    for row_index in range(order - 1, -1, -1):
        unit_row = jnp.where(rows == row_index, 1.0, 0.0).astype(jnp.float32)
        new_row = (
            unit_row - jnp.dot(factor[row_index], inverse, precision=lax.Precision.HIGHEST)
        ) / factor[row_index, row_index]
        inverse = inverse + jnp.where((rows == row_index)[:, None], new_row[None, :], 0.0)
    return inverse


def flip_plane(plane, flip_flag):
    mirror_sign = jnp.array([1.0, -1.0, 1.0], jnp.bfloat16)[:, None, None, None]
    mirrored = plane[:, :, ::-1, :] * mirror_sign
    return jnp.where(flip_flag == 1, mirrored, plane)


def features(x_ext, span_ext, metric):
    half_metric = 0.5 * metric
    interior = x_ext[:, :, 1:-1]
    grad_x = (
        x_ext[:, :, 2:].astype(jnp.float32) - x_ext[:, :, :-2].astype(jnp.float32)
    ) * half_metric[0]
    y_padded = jnp.pad(interior, ((0, 0), (0, 0), (0, 0), (1, 1), (0, 0)))
    grad_y = (
        y_padded[:, :, :, 2:].astype(jnp.float32) - y_padded[:, :, :, :-2].astype(jnp.float32)
    ) * half_metric[1]
    grad_z = (
        span_ext[..., 2:].astype(jnp.float32) - span_ext[..., :-2].astype(jnp.float32)
    ) * half_metric[2]
    vort_x = grad_y[2] - grad_z[1]
    vort_y = grad_z[0] - grad_x[2]
    vort_z = grad_x[1] - grad_y[0]
    q_value = -0.5 * (
        grad_x[0] * grad_x[0]
        + grad_y[1] * grad_y[1]
        + grad_z[2] * grad_z[2]
        + 2.0 * (grad_y[0] * grad_x[1] + grad_z[0] * grad_x[2] + grad_z[1] * grad_y[2])
    )
    weight = lax.rsqrt(metric[0] * metric[1] * metric[2])
    return jnp.stack([vort_x, vort_y, vort_z, q_value]) * weight


def local(velocity, metric, face_flip):
    own_flag = face_flip[0]
    sent_down = flip_plane(velocity[:, :, 0], own_flag)
    above_plane = passed_along(sent_down, "blk", -1)
    below_plane = flip_plane(passed_along(velocity[:, :, -1], "blk", 1), own_flag)
    span_whole = padded(velocity, (("gz", 4),), 1)
    snapshots = velocity.shape[1]
    pieces = []
    for first_snap in range(0, snapshots, 8):
        part_slice = slice(first_snap, first_snap + 8)
        x_ext = jnp.concatenate(
            [
                below_plane[:, part_slice, None],
                velocity[:, part_slice],
                above_plane[:, part_slice, None],
            ],
            axis=2,
        )
        pieces.append(features(x_ext, span_whole[:, part_slice], metric))
    snap_matrix = jnp.concatenate(pieces, axis=1)
    cell_count = float(
        velocity.shape[2]
        * velocity.shape[3]
        * velocity.shape[4]
        * lax.axis_size("blk")
        * lax.axis_size("gz")
    )
    gram_local = jnp.einsum(
        "csxyz,ctxyz->st", snap_matrix, snap_matrix, precision=lax.Precision.HIGHEST
    ) / (4.0 * cell_count)
    gram_whole = lax.psum(gram_local, ("blk", "gz"))
    r_factor = upper_factor(gram_whole)
    r_inverse = upper_inverse(r_factor[:KEEP, :KEEP])
    spatial_modes = jnp.einsum(
        "csxyz,sk->ckxyz", snap_matrix[:, :KEEP], r_inverse, precision=lax.Precision.HIGHEST
    )
    return (spatial_modes, r_factor)


def solution(mesh):
    in_specs = (P(None, None, "blk", None, "gz"), P(None, "blk", None, "gz"), P("blk"))
    out_specs = (P(None, None, "blk", None, "gz"), P())
    return jax.shard_map(local, mesh=mesh, in_specs=in_specs, out_specs=out_specs, check_vma=False)
```

profile of v0, /device:TPU:1, one launch (start us, length us, event | category | flops | bytes accessed | tf_op | source)
XLA Modules:
  0.0 250.2 jit_solution(13199938403154072601)
XLA Ops:
  0.6 3.9 %fusion.272 = (bf16[3,32,4,16,1]{4,3,2,1,0:T(8,128)(2,1)S(1)}, bf16[3,32,4,16,1]{4,3,2,1,0:T(8,128)(2,1)}) fusion(bf16[3,32,4,16,128]{4,3,2,1,0:T(8,128)(2,1)} %param.5), kind=kLoop, calls=%fused_computation.594 | loop fusion | bytes 49152 | tf_op jit(solution)/shard_map/slice | solution.py:24
  4.5 3.6 %copy.66 = bf16[3,32,4,16,1]{1,3,4,2,0:T(8,128)(2,1)} copy(bf16[3,32,4,16,1]{4,3,2,1,0:T(8,128)(2,1)} %get-tuple-element.35) | data formatting | bytes 24576
  8.0 3.5 %collective-permute-start.1 = (bf16[3,32,4,16,1]{1,3,4,2,0:T(8,128)(2,1)}, bf16[3,32,4,16,1]{1,3,4,2,0:T(8,128)(2,1)}, u32[]{:S(2)}, u32[]{:S(2)}) collective-permute-start(bf16[3,32,4,16,1]{1,3,4,2,0:T(8,128)(2,1)} %copy.66), channel_id=1, source_target_pairs={{0,1},{1,2},{2,3},{3,4},{4,5},{5,6},{6,7},{7,8},{8,9},{9,10},{10,1... | collective-permute-start | bytes 36872 | tf_op jit(solution)/shard_map/ppermute | solution.py:21
  11.5 2.4 copy.65
  13.9 3.4 %collective-permute-start = (bf16[3,32,4,16,1]{1,3,4,2,0:T(8,128)(2,1)}, bf16[3,32,4,16,1]{1,3,4,2,0:T(8,128)(2,1)}, u32[]{:S(2)}, u32[]{:S(2)}) collective-permute-start(bf16[3,32,4,16,1]{1,3,4,2,0:T(8,128)(2,1)} %copy.65), channel_id=1, source_target_pairs={{1,0},{2,1},{3,2},{4,3},{5,4},{6,5},{7,6},{8,7},{9,8},{10,9},{11,1... | collective-permute-start | bytes 36872 | tf_op jit(solution)/shard_map/ppermute | solution.py:24
  18.3 2.0 collective-permute-start.3
  41.0 1.0 copy.43
  42.0 1.3 fusion.270
  43.9 0.9 copy.72
  45.4 2.1 copy.48
  47.5 2.9 %copy.46 = bf16[3,32,4,16,1]{4,1,3,2,0:T(8,128)(2,1)} copy(bf16[3,32,4,16,1]{1,3,4,2,0:T(8,128)(2,1)} %collective-permute-done) | data formatting | bytes 24576 | tf_op jit(solution)/shard_map/ppermute | solution.py:24
  50.5 1.8 multiply_select_fusion.1
  52.3 1.5 collective-permute-start.2
  53.8 2.5 %subtract_multiply_fusion.4 = (f32[3,8,4,16,128]{4,1,3,2,0:T(8,128)S(1)}, f32[3,8,4,16,128]{4,1,3,2,0:T(8,128)S(1)}, f32[3,8,4,16,128]{4,1,3,2,0:T(8,128)S(1)}, f32[3,8,4,16,128]{4,1,3,2,0:T(8,128)S(1)}) fusion(bf16[3,32,4,16,128]{4,1,3,2,0:T(8,128)(2,1)S(1)} %copy.43, bf16[3,32,4,16,1]{4,1,3,2,0:T(8,128)(2,1)S(1)} %copy.48, ...), kind=kLoop, calls=%fused_computation.134 | loop fusion | flops 7864320 | bytes 4775936 | tf_op jit(solution)/shard_map/mul | solution.py:72
  56.4 4.4 %collective-permute-done.2 = bf16[3,32,16,128]{3,1,2,0:T(8,128)(2,1)S(1)} collective-permute-done((bf16[3,32,16,128]{3,1,2,0:T(8,128)(2,1)S(1)}, bf16[3,32,16,128]{3,1,2,0:T(8,128)(2,1)S(1)}, u32[]{:S(2)}, u32[]{:S(2)}) %collective-permute-start.2) | collective-permute-done | bytes 393248 | tf_op jit(solution)/shard_map/ppermute | solution.py:12
  64.7 3.4 %fusion.82 = f32[32,32]{1,0:T(8,128)S(1)} fusion(f32[4,8,4,16,128]{4,1,3,2,0:T(8,128)S(1)} %get-tuple-element.61, f32[4,8,4,16,128]{4,1,3,2,0:T(8,128)S(1)} %get-tuple-element.59, f32[4,8,4,16,128]{4,1,3,2,0:T(8,128)S(1)} %get-tuple-element.60, f32[4,8,4,16,128]{4,1,3,2,0:T(8,128)S(1)} %get-tuple-element.62), kind=kOutput, calls=%fused_computation.142 | convolution fusion | flops 405799936 | bytes 4198400 | tf_op jit(solution)/shard_map/csxyz,ctxyz->st/dot_general | solution.py:115
  68.3 107.4 %psum.7 = f32[32,32]{1,0:T(8,128)S(1)} all-reduce(f32[32,32]{1,0:T(8,128)S(1)} %fusion.82), channel_id=1, replica_groups=mesh['blk'=32,'gz'=16] {'blk','gz'}, use_global_device_ids=true, to_apply=%region_0.1 | all-reduce | flops 1024 | bytes 8192 | tf_op jit(solution)/shard_map/psum | solution.py:118
  235.3 0.8 fusion.69
  237.0 0.9 fusion.71
  238.7 0.9 fusion.73
  244.5 0.9 fusion.80
  245.4 0.9 fusion.81
  246.2 1.9 fusion.12
  248.2 2.0 copy.62
  (335 shorter events, 69.8 us)
Async XLA Ops:
  8.0 37.3 %collective-permute-start.1 = (bf16[3,32,4,16,1]{1,3,4,2,0:T(8,128)(2,1)}, bf16[3,32,4,16,1]{1,3,4,2,0:T(8,128)(2,1)}, u32[]{:S(2)}, u32[]{:S(2)}) collective-permute-start(bf16[3,32,4,16,1]{1,3,4,2,0:T(8,128)(2,1)} %copy.66), channel_id=1, source_target_pairs={{0,1},{1,2},{2,3},{3,4},{4,5},{5,6},{6,7},{7,8},{8,9},{9,10},{10,1... | collective-permute-start | bytes 36872 | tf_op jit(solution)/shard_map/ppermute | solution.py:21
  13.9 33.6 %collective-permute-start = (bf16[3,32,4,16,1]{1,3,4,2,0:T(8,128)(2,1)}, bf16[3,32,4,16,1]{1,3,4,2,0:T(8,128)(2,1)}, u32[]{:S(2)}, u32[]{:S(2)}) collective-permute-start(bf16[3,32,4,16,1]{1,3,4,2,0:T(8,128)(2,1)} %copy.65), channel_id=1, source_target_pairs={{1,0},{2,1},{3,2},{4,3},{5,4},{6,5},{7,6},{8,7},{9,8},{10,9},{11,1... | collective-permute-start | bytes 36872 | tf_op jit(solution)/shard_map/ppermute | solution.py:24
  18.3 32.1 %collective-permute-start.3 = (bf16[3,32,16,128]{3,1,2,0:T(8,128)(2,1)}, bf16[3,32,16,128]{3,1,2,0:T(8,128)(2,1)}, u32[]{:S(2)}, u32[]{:S(2)}) collective-permute-start(bf16[3,32,16,128]{3,1,2,0:T(8,128)(2,1)} %bitcast.638), channel_id=1, source_target_pairs={{0,16},{16,32},{32,48},{48,64},{64,80},{80,96},{96,112},{112,128},... | collective-permute-start | bytes 1179656 | tf_op jit(solution)/shard_map/ppermute | solution.py:12
  52.3 8.5 %collective-permute-start.2 = (bf16[3,32,16,128]{3,1,2,0:T(8,128)(2,1)S(1)}, bf16[3,32,16,128]{3,1,2,0:T(8,128)(2,1)S(1)}, u32[]{:S(2)}, u32[]{:S(2)}) collective-permute-start(bf16[3,32,16,128]{3,1,2,0:T(8,128)(2,1)S(1)} %get-tuple-element.79), channel_id=1, source_target_pairs={{16,0},{32,16},{48,32},{64,48},{80,64},{96,80},{112,96},{128,112},... | collective-permute-start | bytes 1179656 | tf_op jit(solution)/shard_map/ppermute | solution.py:12
  68.1 122.2 %copy-start.10 = (pred[32]{0:T(512)(128)(4,1)S(1)}, pred[32]{0:T(512)(128)(4,1)}, u32[]{:S(2)}) copy-start(pred[32]{0:T(512)(128)(4,1)} %iota_compare_fusion.38) | copy-start | bytes 100
  68.1 124.0 %copy-start.13 = (pred[32]{0:T(512)(128)(4,1)S(1)}, pred[32]{0:T(512)(128)(4,1)}, u32[]{:S(2)}) copy-start(pred[32]{0:T(512)(128)(4,1)} %iota_compare_fusion.37) | copy-start | bytes 100
  68.1 125.7 %copy-start.14 = (pred[32]{0:T(512)(128)(4,1)S(1)}, pred[32]{0:T(512)(128)(4,1)}, u32[]{:S(2)}) copy-start(pred[32]{0:T(512)(128)(4,1)} %iota_compare_fusion.36) | copy-start | bytes 100
  68.1 127.5 %copy-start.15 = (pred[32]{0:T(512)(128)(4,1)S(1)}, pred[32]{0:T(512)(128)(4,1)}, u32[]{:S(2)}) copy-start(pred[32]{0:T(512)(128)(4,1)} %iota_compare_fusion.35) | copy-start | bytes 100
  68.2 129.2 %copy-start.16 = (pred[32]{0:T(512)(128)(4,1)S(1)}, pred[32]{0:T(512)(128)(4,1)}, u32[]{:S(2)}) copy-start(pred[32]{0:T(512)(128)(4,1)} %iota_compare_fusion.34) | copy-start | bytes 100
  68.2 131.0 %copy-start.17 = (pred[32]{0:T(512)(128)(4,1)S(1)}, pred[32]{0:T(512)(128)(4,1)}, u32[]{:S(2)}) copy-start(pred[32]{0:T(512)(128)(4,1)} %iota_compare_fusion.33) | copy-start | bytes 100
  68.2 132.7 %copy-start.18 = (pred[32]{0:T(512)(128)(4,1)S(1)}, pred[32]{0:T(512)(128)(4,1)}, u32[]{:S(2)}) copy-start(pred[32]{0:T(512)(128)(4,1)} %iota_compare_fusion.32) | copy-start | bytes 100
  68.2 134.5 %copy-start.19 = (pred[32]{0:T(512)(128)(4,1)S(1)}, pred[32]{0:T(512)(128)(4,1)}, u32[]{:S(2)}) copy-start(pred[32]{0:T(512)(128)(4,1)} %iota_compare_fusion.31) | copy-start | bytes 100
  68.2 136.3 %copy-start.20 = (pred[32]{0:T(512)(128)(4,1)S(1)}, pred[32]{0:T(512)(128)(4,1)}, u32[]{:S(2)}) copy-start(pred[32]{0:T(512)(128)(4,1)} %iota_compare_fusion.30) | copy-start | bytes 100
  68.2 138.1 %copy-start.22 = (pred[32]{0:T(512)(128)(4,1)S(1)}, pred[32]{0:T(512)(128)(4,1)}, u32[]{:S(2)}) copy-start(pred[32]{0:T(512)(128)(4,1)} %iota_compare_fusion.29) | copy-start | bytes 100
  68.2 139.9 %copy-start.23 = (pred[32]{0:T(512)(128)(4,1)S(1)}, pred[32]{0:T(512)(128)(4,1)}, u32[]{:S(2)}) copy-start(pred[32]{0:T(512)(128)(4,1)} %iota_compare_fusion.28) | copy-start | bytes 100
  68.2 141.7 %copy-start.24 = (pred[32]{0:T(512)(128)(4,1)S(1)}, pred[32]{0:T(512)(128)(4,1)}, u32[]{:S(2)}) copy-start(pred[32]{0:T(512)(128)(4,1)} %iota_compare_fusion.27) | copy-start | bytes 100
  68.2 143.5 %copy-start.25 = (pred[32]{0:T(512)(128)(4,1)S(1)}, pred[32]{0:T(512)(128)(4,1)}, u32[]{:S(2)}) copy-start(pred[32]{0:T(512)(128)(4,1)} %iota_compare_fusion.26) | copy-start | bytes 100
  68.2 145.3 %copy-start.26 = (pred[32]{0:T(512)(128)(4,1)S(1)}, pred[32]{0:T(512)(128)(4,1)}, u32[]{:S(2)}) copy-start(pred[32]{0:T(512)(128)(4,1)} %iota_compare_fusion.25) | copy-start | bytes 100
  68.3 147.1 %copy-start.27 = (pred[32]{0:T(512)(128)(4,1)S(1)}, pred[32]{0:T(512)(128)(4,1)}, u32[]{:S(2)}) copy-start(pred[32]{0:T(512)(128)(4,1)} %iota_compare_fusion.24) | copy-start | bytes 100
  68.3 148.9 %copy-start.28 = (pred[32]{0:T(512)(128)(4,1)S(1)}, pred[32]{0:T(512)(128)(4,1)}, u32[]{:S(2)}) copy-start(pred[32]{0:T(512)(128)(4,1)} %iota_compare_fusion.23) | copy-start | bytes 100
  68.3 150.7 %copy-start.30 = (pred[32]{0:T(512)(128)(4,1)S(1)}, pred[32]{0:T(512)(128)(4,1)}, u32[]{:S(2)}) copy-start(pred[32]{0:T(512)(128)(4,1)} %iota_compare_fusion.22) | copy-start | bytes 100
  68.3 152.5 %copy-start.31 = (pred[32]{0:T(512)(128)(4,1)S(1)}, pred[32]{0:T(512)(128)(4,1)}, u32[]{:S(2)}) copy-start(pred[32]{0:T(512)(128)(4,1)} %iota_compare_fusion.21) | copy-start | bytes 100
  68.3 154.4 %copy-start.32 = (pred[32]{0:T(512)(128)(4,1)S(1)}, pred[32]{0:T(512)(128)(4,1)}, u32[]{:S(2)}) copy-start(pred[32]{0:T(512)(128)(4,1)} %iota_compare_fusion.20) | copy-start | bytes 100
  68.3 156.2 %copy-start.33 = (pred[32]{0:T(512)(128)(4,1)S(1)}, pred[32]{0:T(512)(128)(4,1)}, u32[]{:S(2)}) copy-start(pred[32]{0:T(512)(128)(4,1)} %iota_compare_fusion.19) | copy-start | bytes 100
  (34 other events, 1590.6 us)
where the time goes:
time: 251 us; the launch traced here: 250 us
  blocking collectives  107 us (43%)
  local copies, waits for them, and re-layouts  48.2 us (19%)
  other arithmetic  32.5 us (13%)
  between operations  24.2 us (10%)
  matrix products  23.2 us (9%)
  starting transfers between devices  10.4 us (4%)
  waiting for transfers between devices  4.37 us (2%)
    psum x1, blocking collectives, local(): gram_whole = lax.psum(gram_local, ('blk', 'gz'))  107 us
    slice x31, local copies, waits for them, and re-layouts, upper_factor(): pivot = jnp.sqrt(partial_value[column])  18.5 us
    eq x28, other arithmetic, upper_factor(): rows == column  14.1 us
    dot_general x16, matrix products, upper_inverse(): jnp.dot(factor[row_index], inverse, precision=lax.Precision.HIGHEST)  13 us
    unnamed x114, local copies, waits for them, and re-layouts  12.3 us
    eq x10, other arithmetic, upper_inverse(): rows == row_index  5.72 us
    slice x31, local copies, waits for them, and re-layouts, upper_factor(): factor[:, column]  5.52 us
  transfers between devices with their start and end apart: 4, of which 1 were waited for; matrix products, arithmetic and copies ran while one was open for 14% of the time, Pallas kernels for 0%

commit v1 on v0

v1 whole, which is shorter than its diff:
```python
import jax
import jax.numpy as jnp
from jax import lax
from jax.experimental import pallas as pl
from jax.experimental.pallas import tpu as pltpu
from jax.sharding import PartitionSpec as P

KEEP = 16
BF = jnp.bfloat16
F32 = jnp.float32
HIGH = lax.Precision.HIGHEST


def iota(shape, dim):
    return lax.broadcasted_iota(jnp.int32, shape, dim)


def dot(a, b):
    return jnp.dot(a, b, preferred_element_type=F32)


def dot_nt(a, b, precision=None):
    return lax.dot_general(
        a, b, (((1,), (1,)), ((), ())), preferred_element_type=F32, precision=precision
    )


def as_bf(condition):
    return jnp.where(condition, 1.0, 0.0).astype(F32).astype(BF)


def flip_matrix(size, flag):
    row, col = iota((size, size), 0), iota((size, size), 1)
    mirrored = row - (row & 15) + 15 - (row & 15)
    target = jnp.where(flag == 1, mirrored, row)
    return as_bf(col == target)


def split(value):
    high = value.astype(BF)
    low = (value - high.astype(F32)).astype(BF)
    return high, low


def pack_x(flag_ref, vel_ref, down_ref, up_ref, first_ref, sem):
    up = pltpu.make_async_copy(vel_ref.at[:, :, 3], up_ref, sem.at[1])
    first = pltpu.make_async_copy(vel_ref.at[:, :, 0], first_ref, sem.at[0])
    first.start()
    up.start()
    flag = flag_ref[0]
    flip = flip_matrix(256, flag)
    sign = jnp.where(flag == 1, -1.0, 1.0).astype(F32)
    first.wait()
    for comp in range(3):
        for part in range(2):
            rows = pl.ds(16 * part, 16)
            plane = dot(flip, first_ref[comp, rows].reshape(256, 128))
            if comp == 1:
                plane = plane * sign
            down_ref[comp, rows] = plane.astype(BF).reshape(16, 16, 128)
    up.wait()


def pack_z(vel_ref, last_ref, first_ref):
    row, col = iota((128, 256), 0), iota((128, 256), 1)
    pick = as_bf(row == jnp.where(col < 128, 127, 0))
    lane = iota((128, 128), 1)
    last = jnp.zeros((128, 128), F32)
    first = jnp.zeros((128, 128), F32)
    for comp in range(3):
        for x in range(4):
            for part in range(4):
                group = (comp * 4 + x) * 4 + part
                block = vel_ref[comp, pl.ds(8 * part, 8), x].reshape(128, 128)
                ends = dot(block, pick)
                last = jnp.where(lane == group, ends[:, :128], last)
                first = jnp.where(lane == 64 + group, ends[:, 128:], first)
    last_ref[...] = last.astype(BF)
    first_ref[...] = first.astype(BF)


def plane_features(planes, vel_ref, met_ref, low_ref, high_ref, minus, plus, xh_ref, xl_ref, hi, lo):
    row, col = iota((256, 128), 0), iota((256, 128), 1)
    inner = jnp.where(row == col + 1, 1.0, jnp.where(row == col - 1, -1.0, 0.0))
    ends = jnp.where(
        (row >= 192) & (col == 127), 1.0, jnp.where((row < 192) & (col == 0), -1.0, 0.0)
    )
    along_z = jnp.where(row < 128, inner, ends).astype(F32).astype(BF)
    row, col = iota((128, 128), 0), iota((128, 128), 1)
    same = (row >> 4) == (col >> 4)
    along_y = jnp.where(
        same & (col == row + 1), 1.0, jnp.where(same & (col == row - 1), -1.0, 0.0)
    ).astype(F32).astype(BF)
    lane = iota((128, 128), 1)
    halo = low_ref[...] + high_ref[...]

    for place, x in enumerate(planes):
        half_x = (0.5 * met_ref[0, x])[None]
        half_y = (0.5 * met_ref[1, x])[None]
        half_z = (0.5 * met_ref[2, x])[None]
        weight = lax.rsqrt(met_ref[0, x] * met_ref[1, x] * met_ref[2, x])[None]
        for part in range(4):
            snaps = pl.ds(8 * part, 8)
            gx, gy, gz = [], [], []
            for comp in range(3):
                group = (comp * 4 + x) * 4 + part
                block = vel_ref[comp, snaps, x].reshape(128, 128)
                mine = jnp.where((lane & 63) == group, halo, jnp.zeros_like(halo))
                dz = dot(jnp.concatenate([block, mine], axis=1), along_z)
                dy = dot(along_y, block)
                dx = plus(comp, snaps, x) - minus(comp, snaps, x)
                gx.append(dx.reshape(8, 16, 128) * half_x)
                gy.append(dy.reshape(8, 16, 128) * half_y)
                gz.append(dz.reshape(8, 16, 128) * half_z)
            q_value = -0.5 * (gx[0] * gx[0] + gy[1] * gy[1] + gz[2] * gz[2]) - (
                gy[0] * gx[1] + gz[0] * gx[2] + gz[1] * gy[2]
            )
            for feature, value in enumerate(
                (gy[2] - gz[1], gz[0] - gx[2], gx[1] - gy[0], q_value)
            ):
                value = value * weight
                if part < 2:
                    high, low = split(value.reshape(128, 128))
                    rows = pl.ds(128 * part, 128)
                    xh_ref[feature, place, rows] = high
                    xl_ref[feature, place, rows] = low
                for half in range(2):
                    start = ((feature * 2 + place) * 2 + half) * 128
                    high, low = split(value[:, 8 * half : 8 * half + 8].reshape(64, 128))
                    rows = pl.ds(64 * part, 64)
                    hi[rows, start : start + 128] = high
                    lo[rows, start : start + 128] = low


def folded_gram(hi, lo):
    high = hi[...]
    gram = dot_nt(high, high) + 2.0 * dot_nt(high, lo[...])
    row, col = iota((256, 256), 0), iota((256, 256), 1)
    gram = jnp.where((row & 7) == (col & 7), gram, 0.0)
    return jnp.sum(gram.reshape(32, 8, 256), axis=1)


def own_plane(vel_ref, shift):
    def get(comp, snaps, x):
        return vel_ref[comp, snaps, x + shift].astype(F32).reshape(128, 128)

    return get


def inner_kernel(vel_ref, met_ref, low_ref, high_ref, xh_ref, xl_ref, gram_ref, hi, lo):
    plane_features(
        (1, 2), vel_ref, met_ref, low_ref, high_ref, own_plane(vel_ref, -1),
        own_plane(vel_ref, 1), xh_ref, xl_ref, hi, lo,
    )
    gram_ref[...] = folded_gram(hi, lo)


def outer_kernel(
    cells, flag_ref, vel_ref, met_ref, low_ref, high_ref, below_ref, above_ref, inner_ref,
    xh_ref, xl_ref, sent_ref, hi, lo,
):
    flag = flag_ref[0]
    flip = flip_matrix(128, flag)
    sign = jnp.where(flag == 1, -1.0, 1.0).astype(F32)

    def minus(comp, snaps, x):
        if x == 0:
            plane = dot(flip, below_ref[comp, snaps].reshape(128, 128))
            return plane * sign if comp == 1 else plane
        return own_plane(vel_ref, -1)(comp, snaps, x)

    def plus(comp, snaps, x):
        if x == 3:
            return above_ref[comp, snaps].astype(F32).reshape(128, 128)
        return own_plane(vel_ref, 1)(comp, snaps, x)

    plane_features(
        (0, 3), vel_ref, met_ref, low_ref, high_ref, minus, plus, xh_ref, xl_ref, hi, lo
    )
    part = (folded_gram(hi, lo) + inner_ref[...]) * (0.5 / (4.0 * cells))
    row, col = iota((32, 256), 0), iota((32, 256), 1)
    fold = jnp.where(row == (col >> 3), 1.0, 0.0).astype(F32)
    gram = dot_nt(part, fold, HIGH) + dot_nt(fold, part, HIGH)
    first, last = gram[:16], gram[16:]
    row, col = iota((16, 32), 0), iota((16, 32), 1)
    last_moved = jnp.concatenate([last[:, 16:], last[:, :16]], axis=1)
    packed = jnp.where(col >= row, first, last_moved)
    diagonal = jnp.sum(jnp.where(col == row, last_moved, 0.0), axis=0, keepdims=True)
    copies = sent_ref.shape[0]
    for line in range(4):
        text = jnp.concatenate(
            [packed[4 * line + piece : 4 * line + piece + 1] for piece in range(4)], axis=1
        )
        sent_ref[:, :, 128 * line : 128 * line + 128] = jnp.broadcast_to(
            text[None], (copies, 1, 128)
        )
    text = jnp.concatenate([diagonal, jnp.zeros((1, 96), F32)], axis=1)
    sent_ref[:, :, 512:640] = jnp.broadcast_to(text[None], (copies, 1, 128))


def final_kernel(sum_ref, xhi_ref, xli_ref, xho_ref, xlo_ref, modes_ref, r_ref, wh, wl):
    @pl.when(pl.program_id(0) == 0)
    def _():
        pieces = []
        for line in range(16):
            pieces.append(sum_ref[:, 32 * line : 32 * line + 32])
        packed = jnp.concatenate(pieces, axis=0)
        diagonal = sum_ref[:, 512:544]
        row, col = iota((16, 32), 0), iota((16, 32), 1)
        top = jnp.where(col > row, packed, jnp.where(col == row, 0.5 * packed, 0.0))
        low = jnp.where(col < row, packed, jnp.where(col == row, 0.5 * diagonal, 0.0))
        low = jnp.concatenate([low[:, 16:], low[:, :16]], axis=1)
        half = jnp.concatenate([top, low], axis=0)
        row, col = iota((32, 32), 0), iota((32, 32), 1)
        unit = jnp.where(row == col, 1.0, 0.0).astype(F32)
        gram = half + dot_nt(unit, half, HIGH)

        row, col = iota((16, 256), 0), iota((16, 256), 1)
        right = jnp.where(row == (col >> 4), 1.0, 0.0).astype(F32)
        row = iota((32, 1), 0)
        for k in range(32):
            line = gram[k : k + 1]
            factor = jnp.where(row > k, gram[:, k : k + 1] / line[:, k : k + 1], 0.0)
            gram = gram - factor * line
            if k < KEEP - 1:
                right = right - factor[:16] * right[k : k + 1]
        row, col = iota((32, 32), 0), iota((32, 32), 1)
        pivot = jnp.sum(jnp.where(row == col, gram, 0.0), axis=1, keepdims=True)
        scale = 1.0 / jnp.sqrt(pivot)
        r_ref[...] = jnp.where(col >= row, gram * scale, 0.0)
        right = right * scale[:16]
        row, col = iota((256, 256), 0), iota((256, 256), 1)
        wide = jnp.broadcast_to(right[:, None, :], (16, 16, 256)).reshape(256, 256)
        wide = jnp.where((row & 15) == (col & 15), wide, 0.0)
        high, low = split(wide)
        wh[...] = high
        wl[...] = low

    for x, (h_ref, l_ref, place) in enumerate(
        ((xho_ref, xlo_ref, 0), (xhi_ref, xli_ref, 0), (xhi_ref, xli_ref, 1), (xho_ref, xlo_ref, 1))
    ):
        high, low = h_ref[0, place], l_ref[0, place]
        part = dot(wh[...], high) + dot(wh[...], low) + dot(wl[...], high)
        modes_ref[0, :, x] = part.reshape(16, 16, 128)


def vmem():
    return pl.BlockSpec(memory_space=pltpu.VMEM)


def smem():
    return pl.BlockSpec(memory_space=pltpu.SMEM)


def params(mib):
    return pltpu.CompilerParams(vmem_limit_bytes=mib * 2**20)


def local(velocity, metric, face_flip):
    shape = jax.ShapeDtypeStruct
    n_blk, n_gz = lax.axis_size("blk"), lax.axis_size("gz")
    cells = float(4 * 16 * 128 * n_blk * n_gz)
    plane = shape((3, 32, 16, 128), BF)
    sent_down, sent_up = pl.pallas_call(
        pack_x,
        out_shape=(plane, plane),
        in_specs=[smem(), pl.BlockSpec(memory_space=pl.ANY)],
        out_specs=(vmem(), vmem()),
        scratch_shapes=[pltpu.VMEM((3, 32, 16, 128), BF), pltpu.SemaphoreType.DMA((2,))],
        compiler_params=params(16),
    )(face_flip, velocity)
    above = lax.ppermute(sent_down, "blk", [(i + 1, i) for i in range(n_blk - 1)])
    below = lax.ppermute(sent_up, "blk", [(i, i + 1) for i in range(n_blk - 1)])

    side = shape((128, 128), BF)
    last, first = pl.pallas_call(
        pack_z,
        out_shape=(side, side),
        in_specs=[vmem()],
        out_specs=(vmem(), vmem()),
        compiler_params=params(16),
    )(velocity)
    low = lax.ppermute(last, "gz", [(i, (i + 1) % n_gz) for i in range(n_gz)])
    high = lax.ppermute(first, "gz", [((i + 1) % n_gz, i) for i in range(n_gz)])

    half = shape((4, 2, 256, 128), BF)
    scratch = [pltpu.VMEM((256, 2048), BF), pltpu.VMEM((256, 2048), BF)]
    xhi, xli, gram_inner = pl.pallas_call(
        inner_kernel,
        out_shape=(half, half, shape((32, 256), F32)),
        in_specs=[vmem()] * 4,
        out_specs=(vmem(),) * 3,
        scratch_shapes=scratch,
        compiler_params=params(24),
    )(velocity, metric, low, high)

    def outer(*refs):
        outer_kernel(cells, *refs)

    xho, xlo, sent = pl.pallas_call(
        outer,
        out_shape=(half, half, shape((n_gz, 1, 640), F32)),
        in_specs=[smem()] + [vmem()] * 7,
        out_specs=(vmem(),) * 3,
        scratch_shapes=scratch,
        compiler_params=params(24),
    )(face_flip, velocity, metric, low, high, below, above, gram_inner)

    part = jnp.sum(lax.all_to_all(sent, "gz", 0, 0), axis=0)
    part = jnp.broadcast_to(part[None], (n_blk, 1, 640))
    whole = jnp.sum(lax.all_to_all(part, "blk", 0, 0), axis=0)

    piece = pl.BlockSpec((1, 2, 256, 128), lambda i: (i, 0, 0, 0))
    modes, r_factor = pl.pallas_call(
        final_kernel,
        grid=(4,),
        out_shape=(shape((4, 16, 4, 16, 128), F32), shape((32, 32), F32)),
        in_specs=[pl.BlockSpec((1, 640), lambda i: (0, 0))] + [piece] * 4,
        out_specs=(
            pl.BlockSpec((1, 16, 4, 16, 128), lambda i: (i, 0, 0, 0, 0)),
            pl.BlockSpec((32, 32), lambda i: (0, 0)),
        ),
        scratch_shapes=[pltpu.VMEM((256, 256), BF), pltpu.VMEM((256, 256), BF)],
        compiler_params=params(24),
    )(whole, xhi, xli, xho, xlo)
    return (modes, r_factor)


def solution(mesh):
    in_specs = (P(None, None, "blk", None, "gz"), P(None, "blk", None, "gz"), P("blk"))
    out_specs = (P(None, None, "blk", None, "gz"), P())
    return jax.shard_map(local, mesh=mesh, in_specs=in_specs, out_specs=out_specs, check_vma=False)
```

time: 251 us -> 68 us (0.27)
  blocking collectives: 107 us -> 40.6 us
  local copies, waits for them, and re-layouts: 48.2 us -> 1.46 us
  other arithmetic: 32.5 us -> 0.11 us
  matrix products: 23.2 us -> 0 us
  between operations: 24.2 us -> 1.37 us
  Pallas kernels: 0 us -> 12.7 us
    psum x1 -> x0, blocking collectives: 107 us -> none  [local(): gram_whole = lax.psum(gram_local, ('blk', 'gz'))]
    all_to_all x0 -> x2, blocking collectives: none -> 40.6 us  [the longest x1 20.4 us: local(): whole = jnp.sum(lax.all_to_all(part, 'blk', 0, 0), axis=0)]
    slice x66 -> x0, local copies, waits for them, and re-layouts: 30.1 us -> none  [the longest x31 18.5 us: upper_factor(): pivot = jnp.sqrt(partial_value[column])]
    dot_general x50 -> x0, matrix products: 23.2 us -> none  [the longest x16 13 us: upper_inverse(): jnp.dot(factor[row_index], inverse, precision=lax.Precision.HIGHEST)]
    eq x38 -> x0, other arithmetic: 19.9 us -> none  [the longest x28 14.1 us: upper_factor(): rows == column]
    pallas_call x0 -> x5, Pallas kernels: none -> 12.7 us  [the longest x1 6.31 us: local(): pl.pallas_call(final_kernel, grid=(4,), out_shape=(shape((4, 16, 4, 16, 1...]
    unnamed x114 -> x6, local copies, waits for them, and re-layouts: 12.3 us -> 1.41 us
    add x33 -> x0, other arithmetic: 5.06 us -> none  [the longest x31 4.87 us: upper_factor(): factor + jnp.where((rows == column)[:, None], new_row[None, :], 0.0)]
  transfers between devices with their start and end apart: 4 -> 4, of which waited for: 1 -> 2; matrix products, arithmetic and copies ran while one was open for 14% -> 0% of each run, Pallas kernels for 0% -> 5%
where the time goes in v1:
time: 68 us; the launch traced here: 67.7 us
  blocking collectives  40.6 us (60%)
  Pallas kernels  12.7 us (19%)
  starting transfers between devices  9.53 us (14%)
  waiting for transfers between devices  2.02 us (3%)
  local copies, waits for them, and re-layouts  1.46 us (2%)
  between operations  1.37 us (2%)
    all_to_all x1, blocking collectives, local(): whole = jnp.sum(lax.all_to_all(part, 'blk', 0, 0), axis=0)  20.4 us
    all_to_all x1, blocking collectives, local(): part = jnp.sum(lax.all_to_all(sent, 'gz', 0, 0), axis=0)  20.1 us
    pallas_call x1, Pallas kernels, local(): pl.pallas_call(final_kernel, grid=(4,), out_shape=(shape((4, 16, 4, 16, 1...  6.31 us
    ppermute x1, starting transfers between devices, local(): below = lax.ppermute(sent_up, 'blk', [(i, i + 1) for i in range(n_blk - 1)])  3.97 us
    ppermute x1, starting transfers between devices, local(): low = lax.ppermute(last, 'gz', [(i, (i + 1) % n_gz) for i in range(n_gz)])  2.95 us
    pallas_call x1, Pallas kernels, local(): pl.pallas_call(outer, out_shape=(half, half, shape((n_gz, 1, 640), F32)),...  2.65 us
    pallas_call x1, Pallas kernels, local(): pl.pallas_call(inner_kernel, out_shape=(half, half, shape((32, 256), F32)...  2.25 us
    unnamed x6, local copies, waits for them, and re-layouts  1.41 us
  transfers between devices with their start and end apart: 4, of which 2 were waited for; matrix products, arithmetic and copies ran while one was open for 0% of the time, Pallas kernels for 5%

profile of v1, /device:TPU:1, one launch (start us, length us, event | category | flops | bytes accessed | tf_op | source)
XLA Modules:
  0.0 67.7 jit_solution(1740643368382235475)
XLA Ops:
  1.3 0.0 copy-start
  1.3 1.4 %copy-done = bf16[3,32,4,16,128]{4,3,2,1,0:T(8,128)(2,1)S(1)} copy-done((bf16[3,32,4,16,128]{4,3,2,1,0:T(8,128)(2,1)S(1)}, bf16[3,32,4,16,128]{4,3,2,1,0:T(8,128)(2,1)}, u32[]{:S(2)}) %copy-start) | copy-done | bytes 1572888
  2.7 0.0 copy-start.1
  2.7 0.0 copy-start.2
  2.7 0.5 shard_map.51
  3.2 4.0 %collective-permute-start.2 = (bf16[3,32,16,128]{3,2,1,0:T(8,128)(2,1)S(1)}, bf16[3,32,16,128]{3,2,1,0:T(8,128)(2,1)S(1)}, u32[]{:S(2)}, u32[]{:S(2)}) collective-permute-start(bf16[3,32,16,128]{3,2,1,0:T(8,128)(2,1)S(1)} %get-tuple-element.14), channel_id=1, source_target_pairs={{0,16},{16,32},{32,48},{48,64},{64,80},{80,96},{96,112},{112,128},... | collective-permute-start | bytes 1179656 | tf_op jit(solution)/shard_map/ppermute | solution.py:273
  7.2 1.3 %collective-permute-start.3 = (bf16[3,32,16,128]{3,2,1,0:T(8,128)(2,1)S(1)}, bf16[3,32,16,128]{3,2,1,0:T(8,128)(2,1)S(1)}, u32[]{:S(2)}, u32[]{:S(2)}) collective-permute-start(bf16[3,32,16,128]{3,2,1,0:T(8,128)(2,1)S(1)} %get-tuple-element.15), channel_id=1, source_target_pairs={{16,0},{32,16},{48,32},{64,48},{80,64},{96,80},{112,96},{128,112},... | collective-permute-start | bytes 1179656 | tf_op jit(solution)/shard_map/ppermute | solution.py:272
  8.5 1.0 %shard_map.50 = (bf16[128,128]{1,0:T(8,128)(2,1)S(1)}, bf16[128,128]{1,0:T(8,128)(2,1)S(1)}) custom-call(bf16[3,32,4,16,128]{4,3,2,1,0:T(8,128)(2,1)S(1)} %copy-done), custom_call_target="tpu_custom_call" | custom-call | tf_op jit(solution)/shard_map/pallas_call | solution.py:276
  9.5 2.9 %collective-permute-start = (bf16[128,128]{1,0:T(8,128)(2,1)S(1)}, bf16[128,128]{1,0:T(8,128)(2,1)S(1)}, u32[]{:S(2)}, u32[]{:S(2)}) collective-permute-start(bf16[128,128]{1,0:T(8,128)(2,1)S(1)} %get-tuple-element.12), channel_id=1, source_target_pairs={{0,1},{1,2},{2,3},{3,4},{4,5},{5,6},{6,7},{7,8},{8,9},{9,10},{10,1... | collective-permute-start | bytes 98312 | tf_op jit(solution)/shard_map/ppermute | solution.py:283
  12.4 1.3 %collective-permute-start.1 = (bf16[128,128]{1,0:T(8,128)(2,1)S(1)}, bf16[128,128]{1,0:T(8,128)(2,1)S(1)}, u32[]{:S(2)}, u32[]{:S(2)}) collective-permute-start(bf16[128,128]{1,0:T(8,128)(2,1)S(1)} %get-tuple-element.13), channel_id=1, source_target_pairs={{1,0},{2,1},{3,2},{4,3},{5,4},{6,5},{7,6},{8,7},{9,8},{10,9},{11,1... | collective-permute-start | bytes 98312 | tf_op jit(solution)/shard_map/ppermute | solution.py:284
  13.7 0.7 collective-permute-done.low_ref.refs_3_
  14.4 1.3 %collective-permute-done.1.high_ref.refs_4_ = bf16[128,128]{1,0:T(8,128)(2,1)S(1)} collective-permute-done((bf16[128,128]{1,0:T(8,128)(2,1)S(1)}, bf16[128,128]{1,0:T(8,128)(2,1)S(1)}, u32[]{:S(2)}, u32[]{:S(2)}) %collective-permute-start.1) | collective-permute-done | bytes 32800 | tf_op jit(solution)/shard_map/ppermute | solution.py:284
  15.8 0.0 copy-done.1
  15.8 0.0 copy-done.2
  15.8 2.2 %shard_map.52 = (bf16[4,2,256,128]{3,2,1,0:T(8,128)(2,1)S(1)}, bf16[4,2,256,128]{3,2,1,0:T(8,128)(2,1)S(1)}, f32[32,256]{1,0:T(8,128)S(1)}) custom-call(bf16[3,32,4,16,128]{4,3,2,1,0:T(8,128)(2,1)S(1)} %copy-done.1, f32[3,4,16,128]{3,2,1,0:T(8,128)S(1)} %copy-done.2, bf16[128,128]{1,0:T(8,128)(2,1)S(1)} %collective-permute-done.low_ref.refs_3_, ...), custom_call_target="tpu_custom_call" | custom-call | tf_op jit(solution)/shard_map/pallas_call | solution.py:288
  18.0 0.0 collective-permute-done.2.refs_5_
  18.0 0.0 collective-permute-done.3.refs_6_
  18.0 2.7 %shard_map.53 = (bf16[4,2,256,128]{3,2,1,0:T(8,128)(2,1)S(1)}, bf16[4,2,256,128]{3,2,1,0:T(8,128)(2,1)S(1)}, f32[16,1,640]{2,1,0:T(1,128)S(1)}) custom-call(s32[1]{0:T(128)S(6)} %copy.7.flag_ref.refs_0_, bf16[3,32,4,16,128]{4,3,2,1,0:T(8,128)(2,1)S(1)} %copy-done.1, f32[3,4,16,128]{3,2,1,0:T(8,128)S(1)} %copy-done.2, ...), custom_call_target="tpu_custom_call" | custom-call | tf_op jit(solution)/shard_map/pallas_call | solution.py:300
  20.7 20.1 %all_to_all.10 = f32[16,1,640]{2,1,0:T(1,128)S(1)} all-to-all(f32[16,1,640]{2,1,0:T(1,128)S(1)} %get-tuple-element.17), channel_id=1, replica_groups=mesh['blk'=32,'gz'=16] {'gz'}, dimensions={0} | all-to-all | bytes 81920 | tf_op jit(solution)/shard_map/all_to_all | solution.py:309
  40.9 20.4 %all_to_all.11 = f32[32,1,640]{2,1,0:T(1,128)S(1)} all-to-all(f32[32,1,640]{2,1,0:T(1,128)S(1)} %broadcast_in_dim.2), channel_id=1, replica_groups=mesh['blk'=32,'gz'=16] {'blk'}, dimensions={0} | all-to-all | bytes 163840 | tf_op jit(solution)/shard_map/all_to_all | solution.py:311
  61.4 0.1 reduce_sum.21
  61.4 6.3 %shard_map.54 = (f32[4,16,4,16,128]{4,3,2,1,0:T(8,128)}, f32[32,32]{1,0:T(8,128)}) custom-call(f32[1,640]{1,0:T(1,128)S(1)} %reduce_sum.22.sum_ref, bf16[4,2,256,128]{3,2,1,0:T(8,128)(2,1)S(1)} %get-tuple-element.18.xhi_ref, bf16[4,2,256,128]{3,2,1,0:T(8,128)(2,1)S(1)} %get-tuple-element.19.xli_ref, bf16[4,2,256,128]{3,2,1,0:T(8,128)(2,1)S(1)} %get-tuple-element.20.xho_ref, ...), custom_call_target="tpu_custom_call" | custom-call | tf_op jit(solution)/shard_map/pallas_call | solution.py:314
  (3 shorter events, 0.1 us)
Async XLA Ops:
  1.3 1.4 %copy-start = (bf16[3,32,4,16,128]{4,3,2,1,0:T(8,128)(2,1)S(1)}, bf16[3,32,4,16,128]{4,3,2,1,0:T(8,128)(2,1)}, u32[]{:S(2)}) copy-start(bf16[3,32,4,16,128]{4,3,2,1,0:T(8,128)(2,1)} %refs_1_.1) | copy-start | bytes 4718596
  2.7 13.1 %copy-start.1 = (bf16[3,32,4,16,128]{4,3,2,1,0:T(8,128)(2,1)S(1)}, bf16[3,32,4,16,128]{4,3,2,1,0:T(8,128)(2,1)}, u32[]{:S(2)}) copy-start(bf16[3,32,4,16,128]{4,3,2,1,0:T(8,128)(2,1)} %refs_1_.1) | copy-start | bytes 4718596
  2.7 13.1 %copy-start.2 = (f32[3,4,16,128]{3,2,1,0:T(8,128)S(1)}, f32[3,4,16,128]{3,2,1,0:T(8,128)}, u32[]{:S(2)}) copy-start(f32[3,4,16,128]{3,2,1,0:T(8,128)} %refs_2_.1) | copy-start | bytes 294916
  3.2 14.8 %collective-permute-start.2 = (bf16[3,32,16,128]{3,2,1,0:T(8,128)(2,1)S(1)}, bf16[3,32,16,128]{3,2,1,0:T(8,128)(2,1)S(1)}, u32[]{:S(2)}, u32[]{:S(2)}) collective-permute-start(bf16[3,32,16,128]{3,2,1,0:T(8,128)(2,1)S(1)} %get-tuple-element.14), channel_id=1, source_target_pairs={{0,16},{16,32},{32,48},{48,64},{64,80},{80,96},{96,112},{112,128},... | collective-permute-start | bytes 1179656 | tf_op jit(solution)/shard_map/ppermute | solution.py:273
  7.2 10.8 %collective-permute-start.3 = (bf16[3,32,16,128]{3,2,1,0:T(8,128)(2,1)S(1)}, bf16[3,32,16,128]{3,2,1,0:T(8,128)(2,1)S(1)}, u32[]{:S(2)}, u32[]{:S(2)}) collective-permute-start(bf16[3,32,16,128]{3,2,1,0:T(8,128)(2,1)S(1)} %get-tuple-element.15), channel_id=1, source_target_pairs={{16,0},{32,16},{48,32},{64,48},{80,64},{96,80},{112,96},{128,112},... | collective-permute-start | bytes 1179656 | tf_op jit(solution)/shard_map/ppermute | solution.py:272
  9.5 4.9 %collective-permute-start = (bf16[128,128]{1,0:T(8,128)(2,1)S(1)}, bf16[128,128]{1,0:T(8,128)(2,1)S(1)}, u32[]{:S(2)}, u32[]{:S(2)}) collective-permute-start(bf16[128,128]{1,0:T(8,128)(2,1)S(1)} %get-tuple-element.12), channel_id=1, source_target_pairs={{0,1},{1,2},{2,3},{3,4},{4,5},{5,6},{6,7},{7,8},{8,9},{9,10},{10,1... | collective-permute-start | bytes 98312 | tf_op jit(solution)/shard_map/ppermute | solution.py:283
  12.4 3.3 %collective-permute-start.1 = (bf16[128,128]{1,0:T(8,128)(2,1)S(1)}, bf16[128,128]{1,0:T(8,128)(2,1)S(1)}, u32[]{:S(2)}, u32[]{:S(2)}) collective-permute-start(bf16[128,128]{1,0:T(8,128)(2,1)S(1)} %get-tuple-element.13), channel_id=1, source_target_pairs={{1,0},{2,1},{3,2},{4,3},{5,4},{6,5},{7,6},{8,7},{9,8},{10,9},{11,1... | collective-permute-start | bytes 98312 | tf_op jit(solution)/shard_map/ppermute | solution.py:284

commit v2 on v1

v2 whole, which is shorter than its diff:
```python
import jax
import jax.numpy as jnp
from jax import lax
from jax.experimental import pallas as pl
from jax.experimental.pallas import tpu as pltpu
from jax.sharding import PartitionSpec as P

KEEP = 16
BF = jnp.bfloat16
F32 = jnp.float32
HIGH = lax.Precision.HIGHEST


def iota(shape, dim):
    return lax.broadcasted_iota(jnp.int32, shape, dim)


def dot(a, b):
    return jnp.dot(a, b, preferred_element_type=F32)


def dot_nt(a, b, precision=None):
    return lax.dot_general(
        a, b, (((1,), (1,)), ((), ())), preferred_element_type=F32, precision=precision
    )


def as_bf(condition):
    return jnp.where(condition, 1.0, 0.0).astype(F32).astype(BF)


def flip_matrix(size, flag):
    row, col = iota((size, size), 0), iota((size, size), 1)
    mirrored = row - (row & 15) + 15 - (row & 15)
    target = jnp.where(flag == 1, mirrored, row)
    return as_bf(col == target)


def split(value):
    high = value.astype(BF)
    low = (value - high.astype(F32)).astype(BF)
    return high, low


def pack_x(flag_ref, vel_ref, near_ref, far_ref, sem):
    odd = lax.axis_index("blk") & 1
    near = pltpu.make_async_copy(vel_ref.at[:, :, 3 - 3 * odd], near_ref, sem.at[0])
    far = pltpu.make_async_copy(vel_ref.at[:, :, 3 * odd], far_ref, sem.at[1])
    near.start()
    far.start()
    flip = flip_matrix(256, jnp.int32(1))

    def mirror(ref):
        for comp in range(3):
            for part in range(2):
                rows = pl.ds(16 * part, 16)
                plane = dot(flip, ref[comp, rows].reshape(256, 128))
                if comp == 1:
                    plane = -plane
                ref[comp, rows] = plane.astype(BF).reshape(16, 16, 128)

    near.wait()
    far.wait()
    flag = flag_ref[0]

    @pl.when((flag == 1) & (odd == 1))
    def _():
        mirror(near_ref)

    @pl.when((flag == 1) & (odd == 0))
    def _():
        mirror(far_ref)


def pack_z(vel_ref, last_ref, first_ref):
    row, col = iota((128, 256), 0), iota((128, 256), 1)
    pick = as_bf(row == jnp.where(col < 128, 127, 0))
    lane = iota((128, 128), 1)
    last = jnp.zeros((128, 128), F32)
    first = jnp.zeros((128, 128), F32)
    for comp in range(3):
        for x in range(4):
            for part in range(4):
                group = (comp * 4 + x) * 4 + part
                block = vel_ref[comp, pl.ds(8 * part, 8), x].reshape(128, 128)
                ends = dot(block, pick)
                last = jnp.where(lane == group, ends[:, :128], last)
                first = jnp.where(lane == 64 + group, ends[:, 128:], first)
    last_ref[...] = last.astype(BF)
    first_ref[...] = first.astype(BF)


def plane_features(planes, vel_ref, met_ref, low_ref, high_ref, along_x, xh_ref, xl_ref, hi, lo):
    row, col = iota((256, 128), 0), iota((256, 128), 1)
    inner = jnp.where(row == col + 1, 1.0, jnp.where(row == col - 1, -1.0, 0.0))
    ends = jnp.where(
        (row >= 192) & (col == 127), 1.0, jnp.where((row < 192) & (col == 0), -1.0, 0.0)
    )
    along_z = jnp.where(row < 128, inner, ends).astype(F32).astype(BF)
    row, col = iota((128, 128), 0), iota((128, 128), 1)
    same = (row >> 4) == (col >> 4)
    along_y = jnp.where(
        same & (col == row + 1), 1.0, jnp.where(same & (col == row - 1), -1.0, 0.0)
    ).astype(F32).astype(BF)
    lane = iota((128, 128), 1)
    halo = low_ref[...] + high_ref[...]

    for place, x in enumerate(planes):
        half_x = (0.5 * met_ref[0, x])[None]
        half_y = (0.5 * met_ref[1, x])[None]
        half_z = (0.5 * met_ref[2, x])[None]
        weight = lax.rsqrt(met_ref[0, x] * met_ref[1, x] * met_ref[2, x])[None]
        for part in range(4):
            snaps = pl.ds(8 * part, 8)
            gx, gy, gz = [], [], []
            for comp in range(3):
                group = (comp * 4 + x) * 4 + part
                block = vel_ref[comp, snaps, x].reshape(128, 128)
                mine = jnp.where((lane & 63) == group, halo, jnp.zeros_like(halo))
                dz = dot(jnp.concatenate([block, mine], axis=1), along_z)
                dy = dot(along_y, block)
                dx = along_x(comp, snaps, x)
                gx.append(dx.reshape(8, 16, 128) * half_x)
                gy.append(dy.reshape(8, 16, 128) * half_y)
                gz.append(dz.reshape(8, 16, 128) * half_z)
            q_value = -0.5 * (gx[0] * gx[0] + gy[1] * gy[1] + gz[2] * gz[2]) - (
                gy[0] * gx[1] + gz[0] * gx[2] + gz[1] * gy[2]
            )
            for feature, value in enumerate(
                (gy[2] - gz[1], gz[0] - gx[2], gx[1] - gy[0], q_value)
            ):
                value = value * weight
                if part < 2:
                    high, low = split(value.reshape(128, 128))
                    rows = pl.ds(128 * part, 128)
                    xh_ref[feature, place, rows] = high
                    xl_ref[feature, place, rows] = low
                for half in range(2):
                    start = ((feature * len(planes) + place) * 2 + half) * 128
                    high, low = split(value[:, 8 * half : 8 * half + 8].reshape(64, 128))
                    rows = pl.ds(64 * part, 64)
                    hi[rows, start : start + 128] = high
                    lo[rows, start : start + 128] = low


def folded_gram(hi, lo):
    high = hi[...]
    gram = dot_nt(high, high) + 2.0 * dot_nt(high, lo[...])
    row, col = iota((256, 256), 0), iota((256, 256), 1)
    gram = jnp.where((row & 7) == (col & 7), gram, 0.0)
    return jnp.sum(gram.reshape(32, 8, 256), axis=1)


def inner_kernel(vel_ref, met_ref, low_ref, high_ref, xh_ref, xl_ref, gram_ref, hi, lo):
    def along_x(comp, snaps, x):
        after = vel_ref[comp, snaps, x + 1].astype(F32)
        return (after - vel_ref[comp, snaps, x - 1].astype(F32)).reshape(128, 128)

    plane_features(
        (1, 2), vel_ref, met_ref, low_ref, high_ref, along_x, xh_ref, xl_ref, hi, lo
    )
    gram_ref[...] = folded_gram(hi, lo)


def outer_plane(
    far, flag_ref, vel_ref, met_ref, low_ref, high_ref, beside_ref, xh_ref, xl_ref, hi, lo
):
    odd = lax.axis_index("blk") & 1
    is_first = odd if not far else 1 - odd
    flag = flag_ref[0] * is_first
    flip = flip_matrix(128, flag).astype(F32)
    sign = jnp.where(is_first == 1, -1.0, 1.0).astype(F32)
    turned = jnp.where(flag == 1, -1.0, 1.0).astype(F32)
    row, col = iota((128, 128), 0), iota((128, 128), 1)
    unit = jnp.where(row == col, -sign, 0.0).astype(F32)
    straight = jnp.concatenate([flip * sign, unit], axis=1).astype(BF)
    across = jnp.concatenate([flip * (sign * turned), unit], axis=1).astype(BF)

    def along_x(comp, snaps, x):
        both = jnp.concatenate(
            [
                beside_ref[comp, snaps].reshape(128, 128),
                vel_ref[comp, snaps, 2 - is_first].reshape(128, 128),
            ],
            axis=0,
        )
        return dot(across if comp == 1 else straight, both)

    plane_features(
        (3 - 3 * is_first,), vel_ref, met_ref, low_ref, high_ref, along_x, xh_ref, xl_ref, hi, lo
    )
    return folded_gram(hi, lo)


def near_kernel(
    flag_ref, vel_ref, met_ref, low_ref, high_ref, beside_ref, before_ref,
    xh_ref, xl_ref, gram_ref, hi, lo,
):
    gram_ref[...] = before_ref[...] + outer_plane(
        False, flag_ref, vel_ref, met_ref, low_ref, high_ref, beside_ref, xh_ref, xl_ref, hi, lo
    )


def far_kernel(
    cells, flag_ref, vel_ref, met_ref, low_ref, high_ref, beside_ref, before_ref,
    xh_ref, xl_ref, sent_ref, hi, lo,
):
    part = before_ref[...] + outer_plane(
        True, flag_ref, vel_ref, met_ref, low_ref, high_ref, beside_ref, xh_ref, xl_ref, hi, lo
    )
    part = part * (0.5 / (4.0 * cells))
    row, col = iota((32, 256), 0), iota((32, 256), 1)
    fold = jnp.where(row == (col >> 3), 1.0, 0.0).astype(F32)
    gram = dot_nt(part, fold, HIGH) + dot_nt(fold, part, HIGH)
    first, last = gram[:16], gram[16:]
    row, col = iota((16, 32), 0), iota((16, 32), 1)
    last_moved = jnp.concatenate([last[:, 16:], last[:, :16]], axis=1)
    packed = jnp.where(col >= row, first, last_moved)
    diagonal = jnp.sum(jnp.where(col == row, last_moved, 0.0), axis=0, keepdims=True)
    copies = sent_ref.shape[0]
    for line in range(4):
        text = jnp.concatenate(
            [packed[4 * line + piece : 4 * line + piece + 1] for piece in range(4)], axis=1
        )
        sent_ref[:, :, 128 * line : 128 * line + 128] = jnp.broadcast_to(
            text[None], (copies, 1, 128)
        )
    text = jnp.concatenate([diagonal, jnp.zeros((1, 96), F32)], axis=1)
    sent_ref[:, :, 512:640] = jnp.broadcast_to(text[None], (copies, 1, 128))


def wide_row(value, row):
    return jnp.broadcast_to(value[row : row + 1], (8, 128))


def eliminate(first, gram, right):
    home, at = first // 8, first % 8
    cols = [
        [jnp.broadcast_to(g[:, first + j : first + j + 1], (8, 128)) for j in range(4)]
        for g in gram[home:]
    ]
    sides = [[g] for g in gram]
    for i, r in enumerate(right):
        sides[i] += r
    with_right = len(right) > home
    width = len(sides[home])
    lines = [[wide_row(v, at + j) for v in sides[home]] for j in range(4)]
    pivots = [[wide_row(cols[0][m], at + j) for m in range(4)] for j in range(4)]
    ratio = [[None] * 4 for _ in range(4)]
    inverse, root = [], []
    for j in range(4):
        inverse.append(1.0 / pivots[j][j])
        root.append(lax.rsqrt(pivots[j][j]))
        for m in range(j + 1, 4):
            ratio[m][j] = pivots[j][m] * inverse[j]
            for n in range(m, 4):
                pivots[m][n] = pivots[m][n] - ratio[m][j] * pivots[j][n]
            lines[m] = [b - ratio[m][j] * a for a, b in zip(lines[j], lines[m])]
    row = iota((8, 128), 0)
    out_gram, out_right = list(gram), [list(r) for r in right]
    for i in range(home, 4):
        if i == home and at == 4:
            values = list(sides[i])
        else:
            factors = list(cols[i - home])
            for j in range(4):
                for m in range(j + 1, 4):
                    factors[m] = factors[m] - ratio[m][j] * factors[j]
            factors = [f * v for f, v in zip(factors, inverse)]
            values = []
            for n, v in enumerate(sides[i]):
                for j in range(4):
                    v = v - factors[j] * lines[j][n]
                values.append(v)
        if i == home:
            for n in range(width):
                v = jnp.where(row >= at + 4, values[n], sides[i][n])
                for j in range(4):
                    v = jnp.where(row == at + j, lines[j][n] * root[j], v)
                values[n] = v
        out_gram[i] = values[0]
        if i < len(right):
            out_right[i] = values[1:]
    return out_gram, out_right


def final_kernel(
    sum_ref, xhi_ref, xli_ref, xhn_ref, xln_ref, xhf_ref, xlf_ref, modes_ref, r_ref, wide, out, sem
):
    odd = lax.axis_index("blk") & 1
    packed = jnp.concatenate(
        [sum_ref[:, 32 * line : 32 * line + 32] for line in range(16)], axis=0
    )
    diagonal = sum_ref[:, 512:544]
    row, col = iota((16, 32), 0), iota((16, 32), 1)
    top = jnp.where(col > row, packed, jnp.where(col == row, 0.5 * packed, 0.0))
    low = jnp.where(col < row, packed, jnp.where(col == row, 0.5 * diagonal, 0.0))
    low = jnp.concatenate([low[:, 16:], low[:, :16]], axis=1)
    half = jnp.concatenate([top, low], axis=0)
    row, col = iota((32, 32), 0), iota((32, 32), 1)
    unit = jnp.where(row == col, 1.0, 0.0).astype(F32)
    whole = half + dot_nt(unit, half, HIGH)
    whole = jnp.concatenate([whole, jnp.zeros((32, 96), F32)], axis=1)
    gram = [whole[8 * i : 8 * i + 8] for i in range(4)]
    row, col = iota((8, 128), 0), iota((8, 128), 1)
    right = [
        [
            jnp.where(row + 8 * i == (col >> 4) + 8 * side, 1.0, 0.0).astype(F32)
            for side in range(2)
        ]
        for i in range(2)
    ]
    for first in range(0, KEEP, 4):
        gram, right = eliminate(first, gram, right)
    inverse = jnp.concatenate([jnp.concatenate(r, axis=1) for r in right], axis=0)
    row, col = iota((256, 256), 0), iota((256, 256), 1)
    spread = jnp.broadcast_to(inverse[:, None, :], (16, 16, 256)).reshape(256, 256)
    spread = jnp.where((row & 15) == (col & 15), spread, 0.0)
    high, low = split(spread)
    wide[:256] = high
    wide[256:] = low
    for first in range(KEEP, 32, 4):
        gram, _ = eliminate(first, gram, [])
    row, col = iota((32, 32), 0), iota((32, 32), 1)
    whole = jnp.concatenate(gram, axis=0)[:, :32]
    r_ref[...] = jnp.where(col >= row, whole, 0.0)

    places = (3 - 3 * odd, 1, 2, 3 * odd)
    copies = []
    for feature in range(4):
        highs = jnp.concatenate(
            [xhn_ref[feature, 0], xhi_ref[feature, 0], xhi_ref[feature, 1], xhf_ref[feature, 0]], axis=1
        )
        lows = jnp.concatenate(
            [xln_ref[feature, 0], xli_ref[feature, 0], xli_ref[feature, 1], xlf_ref[feature, 0]], axis=1
        )
        both = dot(wide[...], highs)
        modes = both[:256] + both[256:] + dot(wide[:256], lows)
        for n, x in enumerate(places):
            out[feature, :, x] = modes[:, 128 * n : 128 * n + 128].reshape(16, 16, 128)
        copy = pltpu.make_async_copy(out.at[feature], modes_ref.at[feature], sem.at[feature])
        copy.start()
        copies.append(copy)
    for copy in copies:
        copy.wait()


def vmem():
    return pl.BlockSpec(memory_space=pltpu.VMEM)


def smem():
    return pl.BlockSpec(memory_space=pltpu.SMEM)


def params(mib):
    return pltpu.CompilerParams(vmem_limit_bytes=mib * 2**20)


def local(velocity, metric, face_flip):
    shape = jax.ShapeDtypeStruct
    n_blk, n_gz = lax.axis_size("blk"), lax.axis_size("gz")
    cells = float(4 * 16 * 128 * n_blk * n_gz)
    plane = shape((3, 32, 16, 128), BF)
    near_out, far_out = pl.pallas_call(
        pack_x,
        out_shape=(plane, plane),
        in_specs=[smem(), pl.BlockSpec(memory_space=pltpu.HBM)],
        out_specs=(vmem(), vmem()),
        scratch_shapes=[pltpu.SemaphoreType.DMA((2,))],
        compiler_params=params(16),
    )(face_flip, velocity)
    pairs = [(i, i + 1) for i in range(0, n_blk - 1, 2)]
    near_in = lax.ppermute(near_out, "blk", pairs + [(b, a) for a, b in pairs])
    pairs = [(i, i + 1) for i in range(1, n_blk - 1, 2)]
    far_in = lax.ppermute(far_out, "blk", pairs + [(b, a) for a, b in pairs])

    side = shape((128, 128), BF)
    last, first = pl.pallas_call(
        pack_z,
        out_shape=(side, side),
        in_specs=[vmem()],
        out_specs=(vmem(), vmem()),
        compiler_params=params(16),
    )(velocity)
    low = lax.ppermute(last, "gz", [(i, (i + 1) % n_gz) for i in range(n_gz)])
    high = lax.ppermute(first, "gz", [((i + 1) % n_gz, i) for i in range(n_gz)])

    half, quarter = shape((4, 2, 256, 128), BF), shape((4, 1, 256, 128), BF)
    folded = shape((32, 256), F32)
    scratch = [pltpu.VMEM((256, 2048), BF), pltpu.VMEM((256, 2048), BF)]
    xhi, xli, gram = pl.pallas_call(
        inner_kernel,
        out_shape=(half, half, folded),
        in_specs=[vmem()] * 4,
        out_specs=(vmem(),) * 3,
        scratch_shapes=scratch,
        compiler_params=params(24),
    )(velocity, metric, low, high)

    def far_plane(*refs):
        far_kernel(cells, *refs)

    scratch = [pltpu.VMEM((256, 1024), BF), pltpu.VMEM((256, 1024), BF)]
    xhn, xln, gram = pl.pallas_call(
        near_kernel,
        out_shape=(quarter, quarter, folded),
        in_specs=[smem()] + [vmem()] * 6,
        out_specs=(vmem(),) * 3,
        scratch_shapes=scratch,
        compiler_params=params(24),
    )(face_flip, velocity, metric, low, high, near_in, gram)
    xhf, xlf, sent = pl.pallas_call(
        far_plane,
        out_shape=(quarter, quarter, shape((n_gz, 1, 640), F32)),
        in_specs=[smem()] + [vmem()] * 6,
        out_specs=(vmem(),) * 3,
        scratch_shapes=scratch,
        compiler_params=params(24),
    )(face_flip, velocity, metric, low, high, far_in, gram)

    part = jnp.sum(lax.all_to_all(sent, "gz", 0, 0), axis=0)
    part = jnp.broadcast_to(part[None], (n_blk, 1, 640))
    whole = jnp.sum(lax.all_to_all(part, "blk", 0, 0), axis=0)

    modes, r_factor = pl.pallas_call(
        final_kernel,
        out_shape=(shape((4, 16, 4, 16, 128), F32), shape((32, 32), F32)),
        in_specs=[vmem()] * 7,
        out_specs=(pl.BlockSpec(memory_space=pltpu.HBM), vmem()),
        scratch_shapes=[
            pltpu.VMEM((512, 256), BF),
            pltpu.VMEM((4, 16, 4, 16, 128), F32),
            pltpu.SemaphoreType.DMA((4,)),
        ],
        compiler_params=params(24),
    )(whole, xhi, xli, xhn, xln, xhf, xlf)
    return (modes, r_factor)


def solution(mesh):
    in_specs = (P(None, None, "blk", None, "gz"), P(None, "blk", None, "gz"), P("blk"))
    out_specs = (P(None, None, "blk", None, "gz"), P())
    return jax.shard_map(local, mesh=mesh, in_specs=in_specs, out_specs=out_specs, check_vma=False)
```

time: 68 us -> 63.2 us (0.929)
  Pallas kernels: 12.7 us -> 9.71 us
  blocking collectives: 40.6 us -> 38.8 us
    all_to_all x1, blocking collectives: 20.1 us -> 17.1 us  [local(): part = jnp.sum(lax.all_to_all(sent, 'gz', 0, 0), axis=0)]
    pallas_call x3 -> x4, Pallas kernels: 11.2 us -> 8.57 us  [the longest x1 3.35 us: local(): pl.pallas_call(final_kernel, out_shape=(shape((4, 16, 4, 16, 128), F32),...]
    all_to_all x1, blocking collectives: 20.4 us -> 21.6 us  [local(): whole = jnp.sum(lax.all_to_all(part, 'blk', 0, 0), axis=0)]
  transfers between devices with their start and end apart: 4 -> 4, of which waited for: 2 -> 2; matrix products, arithmetic and copies ran while one was open for 0% -> 0% of each run, Pallas kernels for 5% -> 7%
where the time goes in v2:
time: 63.2 us; the launch traced here: 63 us
  blocking collectives  38.8 us (61%)
  Pallas kernels  9.71 us (15%)
  starting transfers between devices  9.65 us (15%)
  waiting for transfers between devices  1.91 us (3%)
  local copies, waits for them, and re-layouts  1.46 us (2%)
  between operations  1.37 us (2%)
    all_to_all x1, blocking collectives, local(): whole = jnp.sum(lax.all_to_all(part, 'blk', 0, 0), axis=0)  21.6 us
    all_to_all x1, blocking collectives, local(): part = jnp.sum(lax.all_to_all(sent, 'gz', 0, 0), axis=0)  17.1 us
    ppermute x1, starting transfers between devices, local(): near_in = lax.ppermute(near_out, 'blk', pairs + [(b, a) for a, b in pairs])  4.3 us
    pallas_call x1, Pallas kernels, local(): pl.pallas_call(final_kernel, out_shape=(shape((4, 16, 4, 16, 128), F32),...  3.35 us
    ppermute x1, starting transfers between devices, local(): low = lax.ppermute(last, 'gz', [(i, (i + 1) % n_gz) for i in range(n_gz)])  2.95 us
    pallas_call x1, Pallas kernels, local(): pl.pallas_call(inner_kernel, out_shape=(half, half, folded), in_specs=[vm...  2.22 us
    ppermute x1, starting transfers between devices, local(): high = lax.ppermute(first, 'gz', [((i + 1) % n_gz, i) for i in range(n_gz)])  1.72 us
    pallas_call x1, Pallas kernels, local(): pl.pallas_call(far_plane, out_shape=(quarter, quarter, shape((n_gz, 1, 64...  1.69 us
  transfers between devices with their start and end apart: 4, of which 2 were waited for; matrix products, arithmetic and copies ran while one was open for 0% of the time, Pallas kernels for 7%

profile of v2, /device:TPU:1, one launch (start us, length us, event | category | flops | bytes accessed | tf_op | source)
XLA Modules:
  0.0 63.0 jit_solution(5898408878937358883)
XLA Ops:
  1.3 0.0 copy-start
  1.3 1.4 %copy-done = bf16[3,32,4,16,128]{4,3,2,1,0:T(8,128)(2,1)S(1)} copy-done((bf16[3,32,4,16,128]{4,3,2,1,0:T(8,128)(2,1)S(1)}, bf16[3,32,4,16,128]{4,3,2,1,0:T(8,128)(2,1)}, u32[]{:S(2)}) %copy-start) | copy-done | bytes 1572888
  2.7 0.0 copy-start.1
  2.7 0.0 copy-start.2
  2.7 0.2 shard_map.51
  2.9 4.3 %collective-permute-start.3 = (bf16[3,32,16,128]{3,2,1,0:T(8,128)(2,1)S(1)}, bf16[3,32,16,128]{3,2,1,0:T(8,128)(2,1)S(1)}, u32[]{:S(2)}, u32[]{:S(2)}) collective-permute-start(bf16[3,32,16,128]{3,2,1,0:T(8,128)(2,1)S(1)} %get-tuple-element.18), channel_id=1, source_target_pairs={{0,16},{32,48},{64,80},{96,112},{128,144},{160,176},{192,208},{224... | collective-permute-start | bytes 1179656 | tf_op jit(solution)/shard_map/ppermute | solution.py:374
  7.2 0.7 %collective-permute-start.2 = (bf16[3,32,16,128]{3,2,1,0:T(8,128)(2,1)S(1)}, bf16[3,32,16,128]{3,2,1,0:T(8,128)(2,1)S(1)}, u32[]{:S(2)}, u32[]{:S(2)}) collective-permute-start(bf16[3,32,16,128]{3,2,1,0:T(8,128)(2,1)S(1)} %get-tuple-element.17), channel_id=1, source_target_pairs={{16,32},{48,64},{80,96},{112,128},{144,160},{176,192},{208,224},{2... | collective-permute-start | bytes 1179656 | tf_op jit(solution)/shard_map/ppermute | solution.py:376
  7.9 1.0 %shard_map.50 = (bf16[128,128]{1,0:T(8,128)(2,1)S(1)}, bf16[128,128]{1,0:T(8,128)(2,1)S(1)}) custom-call(bf16[3,32,4,16,128]{4,3,2,1,0:T(8,128)(2,1)S(1)} %copy-done), custom_call_target="tpu_custom_call" | custom-call | tf_op jit(solution)/shard_map/pallas_call | solution.py:379
  8.8 2.9 %collective-permute-start = (bf16[128,128]{1,0:T(8,128)(2,1)S(1)}, bf16[128,128]{1,0:T(8,128)(2,1)S(1)}, u32[]{:S(2)}, u32[]{:S(2)}) collective-permute-start(bf16[128,128]{1,0:T(8,128)(2,1)S(1)} %get-tuple-element.15), channel_id=1, source_target_pairs={{0,1},{1,2},{2,3},{3,4},{4,5},{5,6},{6,7},{7,8},{8,9},{9,10},{10,1... | collective-permute-start | bytes 98312 | tf_op jit(solution)/shard_map/ppermute | solution.py:386
  11.8 1.7 %collective-permute-start.1 = (bf16[128,128]{1,0:T(8,128)(2,1)S(1)}, bf16[128,128]{1,0:T(8,128)(2,1)S(1)}, u32[]{:S(2)}, u32[]{:S(2)}) collective-permute-start(bf16[128,128]{1,0:T(8,128)(2,1)S(1)} %get-tuple-element.16), channel_id=1, source_target_pairs={{1,0},{2,1},{3,2},{4,3},{5,4},{6,5},{7,6},{8,7},{9,8},{10,9},{11,1... | collective-permute-start | bytes 98312 | tf_op jit(solution)/shard_map/ppermute | solution.py:387
  13.5 0.7 %collective-permute-done.low_ref.refs_3_ = bf16[128,128]{1,0:T(8,128)(2,1)S(1)} collective-permute-done((bf16[128,128]{1,0:T(8,128)(2,1)S(1)}, bf16[128,128]{1,0:T(8,128)(2,1)S(1)}, u32[]{:S(2)}, u32[]{:S(2)}) %collective-permute-start) | collective-permute-done | bytes 32800 | tf_op jit(solution)/shard_map/ppermute | solution.py:386
  14.2 1.2 %collective-permute-done.1.high_ref.refs_4_ = bf16[128,128]{1,0:T(8,128)(2,1)S(1)} collective-permute-done((bf16[128,128]{1,0:T(8,128)(2,1)S(1)}, bf16[128,128]{1,0:T(8,128)(2,1)S(1)}, u32[]{:S(2)}, u32[]{:S(2)}) %collective-permute-start.1) | collective-permute-done | bytes 32800 | tf_op jit(solution)/shard_map/ppermute | solution.py:387
  15.4 0.0 copy-done.1
  15.4 0.0 copy-done.2
  15.4 2.2 %shard_map.52 = (bf16[4,2,256,128]{3,2,1,0:T(8,128)(2,1)S(1)}, bf16[4,2,256,128]{3,2,1,0:T(8,128)(2,1)S(1)}, f32[32,256]{1,0:T(8,128)S(1)}) custom-call(bf16[3,32,4,16,128]{4,3,2,1,0:T(8,128)(2,1)S(1)} %copy-done.1, f32[3,4,16,128]{3,2,1,0:T(8,128)S(1)} %copy-done.2, bf16[128,128]{1,0:T(8,128)(2,1)S(1)} %collective-permute-done.low_ref.refs_3_, ...), custom_call_target="tpu_custom_call" | custom-call | tf_op jit(solution)/shard_map/pallas_call | solution.py:392
  17.7 0.0 collective-permute-done.3.beside_ref
  17.7 1.3 %shard_map.53 = (bf16[4,1,256,128]{3,2,1,0:T(8,128)(2,1)S(1)}, bf16[4,1,256,128]{3,2,1,0:T(8,128)(2,1)S(1)}, f32[32,256]{1,0:T(8,128)S(1)}) custom-call(s32[1]{0:T(128)S(6)} %copy.7.flag_ref.refs_0_, bf16[3,32,4,16,128]{4,3,2,1,0:T(8,128)(2,1)S(1)} %copy-done.1, f32[3,4,16,128]{3,2,1,0:T(8,128)S(1)} %copy-done.2, ...), custom_call_target="tpu_custom_call" | custom-call | tf_op jit(solution)/shard_map/pallas_call | solution.py:405
  19.0 0.0 collective-permute-done.2.refs_5_
  19.0 1.7 %shard_map.54 = (bf16[4,1,256,128]{3,2,1,0:T(8,128)(2,1)S(1)}, bf16[4,1,256,128]{3,2,1,0:T(8,128)(2,1)S(1)}, f32[16,1,640]{2,1,0:T(1,128)S(1)}) custom-call(s32[1]{0:T(128)S(6)} %copy.7.flag_ref.refs_0_, bf16[3,32,4,16,128]{4,3,2,1,0:T(8,128)(2,1)S(1)} %copy-done.1, f32[3,4,16,128]{3,2,1,0:T(8,128)S(1)} %copy-done.2, ...), custom_call_target="tpu_custom_call" | custom-call | tf_op jit(solution)/shard_map/pallas_call | solution.py:413
  20.7 17.1 %all_to_all.10 = f32[16,1,640]{2,1,0:T(1,128)S(1)} all-to-all(f32[16,1,640]{2,1,0:T(1,128)S(1)} %get-tuple-element.21), channel_id=1, replica_groups=mesh['blk'=32,'gz'=16] {'gz'}, dimensions={0} | all-to-all | bytes 81920 | tf_op jit(solution)/shard_map/all_to_all | solution.py:422
  37.9 21.6 %all_to_all.11 = f32[32,1,640]{2,1,0:T(1,128)S(1)} all-to-all(f32[32,1,640]{2,1,0:T(1,128)S(1)} %broadcast_in_dim.2), channel_id=1, replica_groups=mesh['blk'=32,'gz'=16] {'blk'}, dimensions={0} | all-to-all | bytes 163840 | tf_op jit(solution)/shard_map/all_to_all | solution.py:424
  59.6 0.1 reduce_sum.21
  59.6 3.3 %shard_map.55 = (f32[4,16,4,16,128]{4,3,2,1,0:T(8,128)}, f32[32,32]{1,0:T(8,128)}) custom-call(f32[1,640]{1,0:T(1,128)S(1)} %reduce_sum.22.sum_ref, bf16[4,2,256,128]{3,2,1,0:T(8,128)(2,1)S(1)} %get-tuple-element.22.xhi_ref, bf16[4,2,256,128]{3,2,1,0:T(8,128)(2,1)S(1)} %get-tuple-element.23.xli_ref, bf16[4,1,256,128]{3,2,1,0:T(8,128)(2,1)S(1)} %get-tuple-element.24.xhn_ref, ...), custom_call_target="tpu_custom_call" | custom-call | tf_op jit(solution)/shard_map/pallas_call | solution.py:426
  (3 shorter events, 0.1 us)
Async XLA Ops:
  1.3 1.4 %copy-start = (bf16[3,32,4,16,128]{4,3,2,1,0:T(8,128)(2,1)S(1)}, bf16[3,32,4,16,128]{4,3,2,1,0:T(8,128)(2,1)}, u32[]{:S(2)}) copy-start(bf16[3,32,4,16,128]{4,3,2,1,0:T(8,128)(2,1)} %refs_1_.1) | copy-start | bytes 4718596
  2.7 12.7 %copy-start.1 = (bf16[3,32,4,16,128]{4,3,2,1,0:T(8,128)(2,1)S(1)}, bf16[3,32,4,16,128]{4,3,2,1,0:T(8,128)(2,1)}, u32[]{:S(2)}) copy-start(bf16[3,32,4,16,128]{4,3,2,1,0:T(8,128)(2,1)} %refs_1_.1) | copy-start | bytes 4718596
  2.7 12.7 %copy-start.2 = (f32[3,4,16,128]{3,2,1,0:T(8,128)S(1)}, f32[3,4,16,128]{3,2,1,0:T(8,128)}, u32[]{:S(2)}) copy-start(f32[3,4,16,128]{3,2,1,0:T(8,128)} %refs_2_.1) | copy-start | bytes 294916
  2.9 14.8 %collective-permute-start.3 = (bf16[3,32,16,128]{3,2,1,0:T(8,128)(2,1)S(1)}, bf16[3,32,16,128]{3,2,1,0:T(8,128)(2,1)S(1)}, u32[]{:S(2)}, u32[]{:S(2)}) collective-permute-start(bf16[3,32,16,128]{3,2,1,0:T(8,128)(2,1)S(1)} %get-tuple-element.18), channel_id=1, source_target_pairs={{0,16},{32,48},{64,80},{96,112},{128,144},{160,176},{192,208},{224... | collective-permute-start | bytes 1179656 | tf_op jit(solution)/shard_map/ppermute | solution.py:374
  7.2 11.8 %collective-permute-start.2 = (bf16[3,32,16,128]{3,2,1,0:T(8,128)(2,1)S(1)}, bf16[3,32,16,128]{3,2,1,0:T(8,128)(2,1)S(1)}, u32[]{:S(2)}, u32[]{:S(2)}) collective-permute-start(bf16[3,32,16,128]{3,2,1,0:T(8,128)(2,1)S(1)} %get-tuple-element.17), channel_id=1, source_target_pairs={{16,32},{48,64},{80,96},{112,128},{144,160},{176,192},{208,224},{2... | collective-permute-start | bytes 1179656 | tf_op jit(solution)/shard_map/ppermute | solution.py:376
  8.8 5.4 %collective-permute-start = (bf16[128,128]{1,0:T(8,128)(2,1)S(1)}, bf16[128,128]{1,0:T(8,128)(2,1)S(1)}, u32[]{:S(2)}, u32[]{:S(2)}) collective-permute-start(bf16[128,128]{1,0:T(8,128)(2,1)S(1)} %get-tuple-element.15), channel_id=1, source_target_pairs={{0,1},{1,2},{2,3},{3,4},{4,5},{5,6},{6,7},{7,8},{8,9},{9,10},{10,1... | collective-permute-start | bytes 98312 | tf_op jit(solution)/shard_map/ppermute | solution.py:386
  11.8 3.6 %collective-permute-start.1 = (bf16[128,128]{1,0:T(8,128)(2,1)S(1)}, bf16[128,128]{1,0:T(8,128)(2,1)S(1)}, u32[]{:S(2)}, u32[]{:S(2)}) collective-permute-start(bf16[128,128]{1,0:T(8,128)(2,1)S(1)} %get-tuple-element.16), channel_id=1, source_target_pairs={{1,0},{2,1},{3,2},{4,3},{5,4},{6,5},{7,6},{8,7},{9,8},{10,9},{11,1... | collective-permute-start | bytes 98312 | tf_op jit(solution)/shard_map/ppermute | solution.py:387

commit v3 on v2

v3 whole, which is shorter than its diff:
```python
import jax
import jax.numpy as jnp
from jax import lax
from jax.experimental import pallas as pl
from jax.experimental.pallas import tpu as pltpu
from jax.sharding import PartitionSpec as P

KEEP = 16
BF = jnp.bfloat16
F32 = jnp.float32
HIGH = lax.Precision.HIGHEST


def iota(shape, dim):
    return lax.broadcasted_iota(jnp.int32, shape, dim)


def dot(a, b):
    return jnp.dot(a, b, preferred_element_type=F32)


def dot_nt(a, b, precision=None):
    return lax.dot_general(
        a, b, (((1,), (1,)), ((), ())), preferred_element_type=F32, precision=precision
    )


def as_bf(condition):
    return jnp.where(condition, 1.0, 0.0).astype(F32).astype(BF)


def flip_matrix(size, flag):
    row, col = iota((size, size), 0), iota((size, size), 1)
    mirrored = row - (row & 15) + 15 - (row & 15)
    target = jnp.where(flag == 1, mirrored, row)
    return as_bf(col == target)


def split(value):
    high = value.astype(BF)
    low = (value - high.astype(F32)).astype(BF)
    return high, low


def pack_x(flag_ref, vel_ref, near_ref, far_ref, sem):
    even = 1 - (lax.axis_index("blk") & 1)
    near = pltpu.make_async_copy(vel_ref.at[:, :, 3 - 3 * even], near_ref, sem.at[0])
    far = pltpu.make_async_copy(vel_ref.at[:, :, 3 * even], far_ref, sem.at[1])
    near.start()
    far.start()
    flip = flip_matrix(256, jnp.int32(1))

    def mirror(ref):
        for comp in range(3):
            for part in range(2):
                rows = pl.ds(16 * part, 16)
                plane = dot(flip, ref[comp, rows].reshape(256, 128))
                if comp == 1:
                    plane = -plane
                ref[comp, rows] = plane.astype(BF).reshape(16, 16, 128)

    near.wait()
    far.wait()
    flag = flag_ref[0]

    @pl.when((flag == 1) & (even == 1))
    def _():
        mirror(near_ref)

    @pl.when((flag == 1) & (even == 0))
    def _():
        mirror(far_ref)


def pack_z(vel_ref, last_ref, first_ref):
    row, lane = iota((128, 128), 0), iota((128, 128), 1)
    pick = as_bf(row == jnp.where(lane < 64, 127, 0))
    ends = jnp.zeros((128, 128), F32)
    for comp in range(3):
        for x in range(4):
            for part in range(4):
                group = (comp * 4 + x) * 4 + part
                block = vel_ref[comp, pl.ds(8 * part, 8), x].reshape(128, 128)
                ends = jnp.where((lane & 63) == group, dot(block, pick), ends)
    last_ref[...] = jnp.where(lane < 64, ends, 0.0).astype(BF)
    first_ref[...] = jnp.where(lane < 64, 0.0, ends).astype(BF)


def z_matrix():
    row, col = iota((256, 128), 0), iota((256, 128), 1)
    inner = jnp.where(row == col + 1, 1.0, jnp.where(row == col - 1, -1.0, 0.0))
    ends = jnp.where(
        (row >= 192) & (col == 127), 1.0, jnp.where((row < 192) & (col == 0), -1.0, 0.0)
    )
    return jnp.where(row < 128, inner, ends).astype(F32).astype(BF)


def y_matrix():
    row, col = iota((128, 128), 0), iota((128, 128), 1)
    same = (row >> 4) == (col >> 4)
    return jnp.where(
        same & (col == row + 1), 1.0, jnp.where(same & (col == row - 1), -1.0, 0.0)
    ).astype(F32).astype(BF)


def plane_metric(met_ref, x):
    halves = [(0.5 * met_ref[i, x])[None] for i in range(3)]
    return halves, lax.rsqrt(met_ref[0, x] * met_ref[1, x] * met_ref[2, x])[None]


def yz_gradients(vel_ref, halo, along_y, along_z, halves, x, part):
    lane = iota((128, 128), 1)
    blocks, sides = [], []
    for comp in range(3):
        group = (comp * 4 + x) * 4 + part
        blocks.append(vel_ref[comp, pl.ds(8 * part, 8), x].reshape(128, 128))
        sides.append(jnp.where((lane & 63) == group, halo, jnp.zeros_like(halo)))
    dz = dot(
        jnp.concatenate([jnp.concatenate(blocks, axis=0), jnp.concatenate(sides, axis=0)], axis=1),
        along_z,
    )
    dy = dot(along_y, jnp.concatenate(blocks, axis=1))
    gy = [dy[:, 128 * i : 128 * i + 128].reshape(8, 16, 128) * halves[1] for i in range(3)]
    gz = [dz[128 * i : 128 * i + 128].reshape(8, 16, 128) * halves[2] for i in range(3)]
    return gy, gz


def store_feature(value, part, slot, xh_ref, xl_ref, index, hi, lo):
    if part < 2:
        high, low = split(value.reshape(128, 128))
        rows = pl.ds(128 * part, 128)
        xh_ref[*index, rows] = high
        xl_ref[*index, rows] = low
    for half in range(2):
        start = (slot * 2 + half) * 128
        high, low = split(value[:, 8 * half : 8 * half + 8].reshape(64, 128))
        rows = pl.ds(64 * part, 64)
        hi[rows, start : start + 128] = high
        lo[rows, start : start + 128] = low


def folded_gram(hi, lo):
    high = hi[...]
    gram = dot_nt(high, high) + 2.0 * dot_nt(high, lo[...])
    row, col = iota((256, 256), 0), iota((256, 256), 1)
    gram = jnp.where((row & 7) == (col & 7), gram, 0.0)
    return jnp.sum(gram.reshape(32, 8, 256), axis=1)


def inner_kernel(
    vel_ref, met_ref, low_ref, high_ref,
    xh_ref, xl_ref, xhs_ref, xls_ref, side_ref, gram_ref, hi, lo,
):
    along_y, along_z = y_matrix(), z_matrix()
    halo = low_ref[...] + high_ref[...]
    for place, x in enumerate((1, 2)):
        halves, weight = plane_metric(met_ref, x)
        for part in range(4):
            gy, gz = yz_gradients(vel_ref, halo, along_y, along_z, halves, x, part)
            snaps = pl.ds(8 * part, 8)
            gx = []
            for comp in range(3):
                after = vel_ref[comp, snaps, x + 1].astype(F32)
                gx.append((after - vel_ref[comp, snaps, x - 1].astype(F32)) * halves[0])
            q_value = -0.5 * (gx[0] * gx[0] + gy[1] * gy[1] + gz[2] * gz[2]) - (
                gy[0] * gx[1] + gz[0] * gx[2] + gz[1] * gy[2]
            )
            for feature, value in enumerate(
                (gy[2] - gz[1], gz[0] - gx[2], gx[1] - gy[0], q_value)
            ):
                store_feature(
                    value * weight, part, feature * 2 + place, xh_ref, xl_ref, (feature, place), hi, lo
                )
    for place, x in enumerate((0, 3)):
        halves, weight = plane_metric(met_ref, x)
        for part in range(4):
            gy, gz = yz_gradients(vel_ref, halo, along_y, along_z, halves, x, part)
            store_feature(
                (gy[2] - gz[1]) * weight, part, 8 + place, xhs_ref, xls_ref, (place,), hi, lo
            )
            snaps = pl.ds(8 * part, 8)
            side_ref[place, 0, snaps] = gy[0]
            side_ref[place, 1, snaps] = gz[0]
            side_ref[place, 2, snaps] = -0.5 * (gy[1] * gy[1] + gz[2] * gz[2]) - gz[1] * gy[2]
    gram_ref[...] = folded_gram(hi, lo)


def outer_plane(far, flag_ref, vel_ref, met_ref, side_ref, beside_ref, xh_ref, xl_ref, hi, lo):
    even = 1 - (lax.axis_index("blk") & 1)
    is_first = even if not far else 1 - even
    x, place = 3 - 3 * is_first, 1 - is_first
    flag = flag_ref[0] * is_first
    flip = flip_matrix(128, flag).astype(F32)
    sign = jnp.where(is_first == 1, -1.0, 1.0).astype(F32)
    turned = jnp.where(flag == 1, -1.0, 1.0).astype(F32)
    row, col = iota((128, 128), 0), iota((128, 128), 1)
    unit = jnp.where(row == col, -sign, 0.0).astype(F32)
    straight = jnp.concatenate([flip * sign, unit], axis=1).astype(BF)
    across = jnp.concatenate([flip * (sign * turned), unit], axis=1).astype(BF)
    halves, weight = plane_metric(met_ref, x)
    for part in range(4):
        snaps = pl.ds(8 * part, 8)
        gx = []
        for comp in range(3):
            both = jnp.concatenate(
                [
                    beside_ref[comp, snaps].reshape(128, 128),
                    vel_ref[comp, snaps, 2 - is_first].reshape(128, 128),
                ],
                axis=0,
            )
            dx = dot(across if comp == 1 else straight, both)
            gx.append(dx.reshape(8, 16, 128) * halves[0])
        gy0, gz0 = side_ref[place, 0, snaps], side_ref[place, 1, snaps]
        q_value = side_ref[place, 2, snaps] - 0.5 * (gx[0] * gx[0]) - (gy0 * gx[1] + gz0 * gx[2])
        for feature, value in enumerate((gz0 - gx[2], gx[1] - gy0, q_value)):
            store_feature(value * weight, part, feature, xh_ref, xl_ref, (feature,), hi, lo)
    return folded_gram(hi, lo)


def near_kernel(
    flag_ref, vel_ref, met_ref, side_ref, beside_ref, before_ref, xh_ref, xl_ref, gram_ref, hi, lo
):
    gram_ref[...] = before_ref[...] + outer_plane(
        False, flag_ref, vel_ref, met_ref, side_ref, beside_ref, xh_ref, xl_ref, hi, lo
    )


def far_kernel(
    cells, flag_ref, vel_ref, met_ref, side_ref, beside_ref, before_ref, xh_ref, xl_ref, sent_ref, hi, lo
):
    part = before_ref[...] + outer_plane(
        True, flag_ref, vel_ref, met_ref, side_ref, beside_ref, xh_ref, xl_ref, hi, lo
    )
    part = part * (0.5 / (4.0 * cells))
    row, col = iota((32, 256), 0), iota((32, 256), 1)
    fold = as_bf(row == (col >> 3))
    fold = jnp.concatenate([fold] * 3, axis=1)
    high, low = split(part)
    rest = (part - high.astype(F32) - low.astype(F32)).astype(BF)
    part = jnp.concatenate([high, low, rest], axis=1)
    gram = dot_nt(part, fold) + dot_nt(fold, part)
    first, last = gram[:16], gram[16:]
    row, col = iota((16, 32), 0), iota((16, 32), 1)
    last_moved = jnp.concatenate([last[:, 16:], last[:, :16]], axis=1)
    packed = jnp.where(col >= row, first, last_moved)
    diagonal = jnp.sum(jnp.where(col == row, last_moved, 0.0), axis=0, keepdims=True)
    copies = sent_ref.shape[0]
    for line in range(4):
        text = jnp.concatenate(
            [packed[4 * line + piece : 4 * line + piece + 1] for piece in range(4)], axis=1
        )
        sent_ref[:, :, 128 * line : 128 * line + 128] = jnp.broadcast_to(
            text[None], (copies, 1, 128)
        )
    text = jnp.concatenate([diagonal, jnp.zeros((1, 96), F32)], axis=1)
    sent_ref[:, :, 512:640] = jnp.broadcast_to(text[None], (copies, 1, 128))


def wide_row(value, row):
    return jnp.broadcast_to(value[row : row + 1], (8, 128))


def eliminate(first, gram, right):
    home, at = first // 8, first % 8
    cols = [
        [jnp.broadcast_to(g[:, first + j : first + j + 1], (8, 128)) for j in range(4)]
        for g in gram[home:]
    ]
    sides = [[g] for g in gram]
    for i, r in enumerate(right):
        sides[i] += r
    with_right = len(right) > home
    width = len(sides[home])
    lines = [[wide_row(v, at + j) for v in sides[home]] for j in range(4)]
    pivots = [[wide_row(cols[0][m], at + j) for m in range(4)] for j in range(4)]
    ratio = [[None] * 4 for _ in range(4)]
    inverse, root = [], []
    for j in range(4):
        inverse.append(1.0 / pivots[j][j])
        root.append(lax.rsqrt(pivots[j][j]))
        for m in range(j + 1, 4):
            ratio[m][j] = pivots[j][m] * inverse[j]
            for n in range(m, 4):
                pivots[m][n] = pivots[m][n] - ratio[m][j] * pivots[j][n]
            lines[m] = [b - ratio[m][j] * a for a, b in zip(lines[j], lines[m])]
    row = iota((8, 128), 0)
    out_gram, out_right = list(gram), [list(r) for r in right]
    for i in range(home, 4):
        if i == home and at == 4:
            values = list(sides[i])
        else:
            factors = list(cols[i - home])
            for j in range(4):
                for m in range(j + 1, 4):
                    factors[m] = factors[m] - ratio[m][j] * factors[j]
            factors = [f * v for f, v in zip(factors, inverse)]
            values = []
            for n, v in enumerate(sides[i]):
                for j in range(4):
                    v = v - factors[j] * lines[j][n]
                values.append(v)
        if i == home:
            for n in range(width):
                v = jnp.where(row >= at + 4, values[n], sides[i][n])
                for j in range(4):
                    v = jnp.where(row == at + j, lines[j][n] * root[j], v)
                values[n] = v
        out_gram[i] = values[0]
        if i < len(right):
            out_right[i] = values[1:]
    return out_gram, out_right


def final_kernel(
    sum_ref, xhi_ref, xli_ref, xhs_ref, xls_ref, xhn_ref, xln_ref, xhf_ref, xlf_ref,
    modes_ref, r_ref, wide, out, sem,
):
    even = 1 - (lax.axis_index("blk") & 1)
    packed = jnp.concatenate(
        [sum_ref[:, 32 * line : 32 * line + 32] for line in range(16)], axis=0
    )
    diagonal = sum_ref[:, 512:544]
    row, col = iota((16, 32), 0), iota((16, 32), 1)
    top = jnp.where(col > row, packed, jnp.where(col == row, 0.5 * packed, 0.0))
    low = jnp.where(col < row, packed, jnp.where(col == row, 0.5 * diagonal, 0.0))
    low = jnp.concatenate([low[:, 16:], low[:, :16]], axis=1)
    half = jnp.concatenate([top, low], axis=0)
    row, col = iota((32, 32), 0), iota((32, 32), 1)
    unit = jnp.where(row == col, 1.0, 0.0).astype(F32)
    whole = half + dot_nt(unit, half, HIGH)
    whole = jnp.concatenate([whole, jnp.zeros((32, 96), F32)], axis=1)
    gram = [whole[8 * i : 8 * i + 8] for i in range(4)]
    row, col = iota((8, 128), 0), iota((8, 128), 1)
    right = [
        [
            jnp.where(row + 8 * i == (col >> 4) + 8 * side, 1.0, 0.0).astype(F32)
            for side in range(2)
        ]
        for i in range(2)
    ]
    for first in range(0, KEEP, 4):
        gram, right = eliminate(first, gram, right)
    inverse = jnp.concatenate([jnp.concatenate(r, axis=1) for r in right], axis=0)
    row, col = iota((256, 256), 0), iota((256, 256), 1)
    spread = jnp.broadcast_to(inverse[:, None, :], (16, 16, 256)).reshape(256, 256)
    spread = jnp.where((row & 15) == (col & 15), spread, 0.0)
    high, low = split(spread)
    wide[:256] = high
    wide[256:] = low
    copies = []
    for feature in range(4):
        if feature == 0:
            places = (0, 1, 2, 3)
            pieces = [(xhs_ref[0], xls_ref[0]), (xhs_ref[1], xls_ref[1])]
        else:
            places = (3 - 3 * even, 1, 2, 3 * even)
            pieces = [
                (xhn_ref[feature - 1], xln_ref[feature - 1]),
                (xhf_ref[feature - 1], xlf_ref[feature - 1]),
            ]
        for place in (1, 0):
            pieces.insert(1, (xhi_ref[feature, place], xli_ref[feature, place]))
        highs = jnp.concatenate([piece[0] for piece in pieces], axis=1)
        lows = jnp.concatenate([piece[1] for piece in pieces], axis=1)
        both = dot(wide[...], highs)
        modes = both[:256] + both[256:] + dot(wide[:256], lows)
        for n, x in enumerate(places):
            out[feature, :, x] = modes[:, 128 * n : 128 * n + 128].reshape(16, 16, 128)
        gram, _ = eliminate(KEEP + 4 * feature, gram, [])
        copy = pltpu.make_async_copy(out.at[feature], modes_ref.at[feature], sem.at[feature])
        copy.start()
        copies.append(copy)
    row, col = iota((32, 32), 0), iota((32, 32), 1)
    whole = jnp.concatenate(gram, axis=0)[:, :32]
    r_ref[...] = jnp.where(col >= row, whole, 0.0)
    for copy in copies:
        copy.wait()


def vmem():
    return pl.BlockSpec(memory_space=pltpu.VMEM)


def smem():
    return pl.BlockSpec(memory_space=pltpu.SMEM)


def params(mib):
    return pltpu.CompilerParams(vmem_limit_bytes=mib * 2**20)


def local(velocity, metric, face_flip):
    shape = jax.ShapeDtypeStruct
    n_blk, n_gz = lax.axis_size("blk"), lax.axis_size("gz")
    cells = float(4 * 16 * 128 * n_blk * n_gz)
    plane = shape((3, 32, 16, 128), BF)
    near_out, far_out = pl.pallas_call(
        pack_x,
        out_shape=(plane, plane),
        in_specs=[smem(), pl.BlockSpec(memory_space=pltpu.HBM)],
        out_specs=(vmem(), vmem()),
        scratch_shapes=[pltpu.SemaphoreType.DMA((2,))],
        compiler_params=params(16),
    )(face_flip, velocity)
    pairs = [(i, i + 1) for i in range(1, n_blk - 1, 2)]
    near_in = lax.ppermute(near_out, "blk", pairs + [(b, a) for a, b in pairs])
    pairs = [(i, i + 1) for i in range(0, n_blk - 1, 2)]
    far_in = lax.ppermute(far_out, "blk", pairs + [(b, a) for a, b in pairs])

    side = shape((128, 128), BF)
    last, first = pl.pallas_call(
        pack_z,
        out_shape=(side, side),
        in_specs=[vmem()],
        out_specs=(vmem(), vmem()),
        compiler_params=params(16),
    )(velocity)
    low = lax.ppermute(last, "gz", [(i, (i + 1) % n_gz) for i in range(n_gz)])
    high = lax.ppermute(first, "gz", [((i + 1) % n_gz, i) for i in range(n_gz)])

    half, outer, side = shape((4, 2, 256, 128), BF), shape((3, 256, 128), BF), shape((2, 256, 128), BF)
    folded = shape((32, 256), F32)
    xhi, xli, xhs, xls, sides, gram = pl.pallas_call(
        inner_kernel,
        out_shape=(half, half, side, side, shape((2, 3, 32, 16, 128), F32), folded),
        in_specs=[vmem()] * 4,
        out_specs=(vmem(),) * 6,
        scratch_shapes=[pltpu.VMEM((256, 2560), BF), pltpu.VMEM((256, 2560), BF)],
        compiler_params=params(24),
    )(velocity, metric, low, high)

    def far_plane(*refs):
        far_kernel(cells, *refs)

    scratch = [pltpu.VMEM((256, 768), BF), pltpu.VMEM((256, 768), BF)]
    xhn, xln, gram = pl.pallas_call(
        near_kernel,
        out_shape=(outer, outer, folded),
        in_specs=[smem()] + [vmem()] * 5,
        out_specs=(vmem(),) * 3,
        scratch_shapes=scratch,
        compiler_params=params(24),
    )(face_flip, velocity, metric, sides, near_in, gram)
    xhf, xlf, sent = pl.pallas_call(
        far_plane,
        out_shape=(outer, outer, shape((n_gz, 1, 640), F32)),
        in_specs=[smem()] + [vmem()] * 5,
        out_specs=(vmem(),) * 3,
        scratch_shapes=scratch,
        compiler_params=params(24),
    )(face_flip, velocity, metric, sides, far_in, gram)

    part = jnp.sum(lax.all_to_all(sent, "gz", 0, 0), axis=0)
    part = jnp.broadcast_to(part[None], (n_blk, 1, 640))
    whole = jnp.sum(lax.all_to_all(part, "blk", 0, 0), axis=0)

    modes, r_factor = pl.pallas_call(
        final_kernel,
        out_shape=(shape((4, 16, 4, 16, 128), F32), shape((32, 32), F32)),
        in_specs=[vmem()] * 9,
        out_specs=(pl.BlockSpec(memory_space=pltpu.HBM), vmem()),
        scratch_shapes=[
            pltpu.VMEM((512, 256), BF),
            pltpu.VMEM((4, 16, 4, 16, 128), F32),
            pltpu.SemaphoreType.DMA((4,)),
        ],
        compiler_params=params(24),
    )(whole, xhi, xli, xhs, xls, xhn, xln, xhf, xlf)
    return (modes, r_factor)


def solution(mesh):
    in_specs = (P(None, None, "blk", None, "gz"), P(None, "blk", None, "gz"), P("blk"))
    out_specs = (P(None, None, "blk", None, "gz"), P())
    return jax.shard_map(local, mesh=mesh, in_specs=in_specs, out_specs=out_specs, check_vma=False)
```

time: 63.2 us -> 61.3 us (0.970)
  blocking collectives: 38.8 us -> 34.7 us
  waiting for transfers between devices: 1.91 us -> 3.64 us
  starting transfers between devices: 9.65 us -> 10.3 us
    ppermute x1, starting transfers between devices: 0.69 us -> 6.38 us  [local(): far_in = lax.ppermute(far_out, 'blk', pairs + [(b, a) for a, b in pairs])]
    all_to_all x1, blocking collectives: 21.6 us -> 17.9 us  [local(): whole = jnp.sum(lax.all_to_all(part, 'blk', 0, 0), axis=0)]
    ppermute x1, starting transfers between devices: 4.3 us -> 0.69 us  [local(): near_in = lax.ppermute(near_out, 'blk', pairs + [(b, a) for a, b in pairs])]
    ppermute x1, starting transfers between devices: 1.72 us -> 0.01 us  [local(): high = lax.ppermute(first, 'gz', [((i + 1) % n_gz, i) for i in range(n_gz)])]
    ppermute x1, waiting for transfers between devices: 1.23 us -> 2.61 us  [local(): high = lax.ppermute(first, 'gz', [((i + 1) % n_gz, i) for i in range(n_gz)])]
where the time goes in v3:
time: 61.3 us; the launch traced here: 61 us
  blocking collectives  34.7 us (57%)
  starting transfers between devices  10.3 us (17%)
  Pallas kernels  9.46 us (15%)
  waiting for transfers between devices  3.64 us (6%)
  local copies, waits for them, and re-layouts  1.46 us (2%)
  between operations  1.37 us (2%)
    all_to_all x1, blocking collectives, local(): whole = jnp.sum(lax.all_to_all(part, 'blk', 0, 0), axis=0)  17.9 us
    all_to_all x1, blocking collectives, local(): part = jnp.sum(lax.all_to_all(sent, 'gz', 0, 0), axis=0)  16.7 us
    ppermute x1, starting transfers between devices, local(): far_in = lax.ppermute(far_out, 'blk', pairs + [(b, a) for a, b in pairs])  6.38 us
    pallas_call x1, Pallas kernels, local(): pl.pallas_call(final_kernel, out_shape=(shape((4, 16, 4, 16, 128), F32),...  3.35 us
    ppermute x1, starting transfers between devices, local(): low = lax.ppermute(last, 'gz', [(i, (i + 1) % n_gz) for i in range(n_gz)])  3.23 us
    pallas_call x1, Pallas kernels, local(): pl.pallas_call(inner_kernel, out_shape=(half, half, side, side, shape((2,...  2.85 us
    ppermute x1, waiting for transfers between devices, local(): high = lax.ppermute(first, 'gz', [((i + 1) % n_gz, i) for i in range(n_gz)])  2.61 us
    unnamed x6, local copies, waits for them, and re-layouts  1.41 us
  transfers between devices with their start and end apart: 4, of which 2 were waited for; matrix products, arithmetic and copies ran while one was open for 0% of the time, Pallas kernels for 7%

profile of v3, /device:TPU:1, one launch (start us, length us, event | category | flops | bytes accessed | tf_op | source)
XLA Modules:
  0.0 61.0 jit_solution(15833122006712817897)
XLA Ops:
  1.3 0.0 copy-start
  1.3 1.4 %copy-done = bf16[3,32,4,16,128]{4,3,2,1,0:T(8,128)(2,1)S(1)} copy-done((bf16[3,32,4,16,128]{4,3,2,1,0:T(8,128)(2,1)S(1)}, bf16[3,32,4,16,128]{4,3,2,1,0:T(8,128)(2,1)}, u32[]{:S(2)}) %copy-start) | copy-done | bytes 1572888
  2.7 0.0 copy-start.1
  2.7 0.0 copy-start.2
  2.7 0.5 shard_map.52
  3.2 0.7 %collective-permute-start.3 = (bf16[3,32,16,128]{3,2,1,0:T(8,128)(2,1)S(1)}, bf16[3,32,16,128]{3,2,1,0:T(8,128)(2,1)S(1)}, u32[]{:S(2)}, u32[]{:S(2)}) collective-permute-start(bf16[3,32,16,128]{3,2,1,0:T(8,128)(2,1)S(1)} %get-tuple-element.22), channel_id=1, source_target_pairs={{16,32},{48,64},{80,96},{112,128},{144,160},{176,192},{208,224},{2... | collective-permute-start | bytes 1179656 | tf_op jit(solution)/shard_map/ppermute | solution.py:407
  3.9 6.4 %collective-permute-start.2 = (bf16[3,32,16,128]{3,2,1,0:T(8,128)(2,1)S(1)}, bf16[3,32,16,128]{3,2,1,0:T(8,128)(2,1)S(1)}, u32[]{:S(2)}, u32[]{:S(2)}) collective-permute-start(bf16[3,32,16,128]{3,2,1,0:T(8,128)(2,1)S(1)} %get-tuple-element.21), channel_id=1, source_target_pairs={{0,16},{32,48},{64,80},{96,112},{128,144},{160,176},{192,208},{224... | collective-permute-start | bytes 1179656 | tf_op jit(solution)/shard_map/ppermute | solution.py:409
  10.3 0.6 shard_map.50
  10.9 3.2 %collective-permute-start = (bf16[128,128]{1,0:T(8,128)(2,1)S(1)}, bf16[128,128]{1,0:T(8,128)(2,1)S(1)}, u32[]{:S(2)}, u32[]{:S(2)}) collective-permute-start(bf16[128,128]{1,0:T(8,128)(2,1)S(1)} %get-tuple-element.18), channel_id=1, source_target_pairs={{0,1},{1,2},{2,3},{3,4},{4,5},{5,6},{6,7},{7,8},{8,9},{9,10},{10,1... | collective-permute-start | bytes 98312 | tf_op jit(solution)/shard_map/ppermute | solution.py:419
  14.1 0.0 collective-permute-start.1
  14.1 1.0 %collective-permute-done.low_ref = bf16[128,128]{1,0:T(8,128)(2,1)S(1)} collective-permute-done((bf16[128,128]{1,0:T(8,128)(2,1)S(1)}, bf16[128,128]{1,0:T(8,128)(2,1)S(1)}, u32[]{:S(2)}, u32[]{:S(2)}) %collective-permute-start) | collective-permute-done | bytes 32800 | tf_op jit(solution)/shard_map/ppermute | solution.py:419
  15.1 2.6 %collective-permute-done.1.high_ref = bf16[128,128]{1,0:T(8,128)(2,1)S(1)} collective-permute-done((bf16[128,128]{1,0:T(8,128)(2,1)S(1)}, bf16[128,128]{1,0:T(8,128)(2,1)S(1)}, u32[]{:S(2)}, u32[]{:S(2)}) %collective-permute-start.1) | collective-permute-done | bytes 32800 | tf_op jit(solution)/shard_map/ppermute | solution.py:420
  17.7 0.0 copy-done.1
  17.7 0.0 copy-done.2
  17.7 2.8 %shard_map.51 = (bf16[4,2,256,128]{3,2,1,0:T(8,128)(2,1)S(1)}, bf16[4,2,256,128]{3,2,1,0:T(8,128)(2,1)S(1)}, bf16[2,256,128]{2,1,0:T(8,128)(2,1)S(1)}, bf16[2,25...) custom-call(bf16[3,32,4,16,128]{4,3,2,1,0:T(8,128)(2,1)S(1)} %copy-done.1, ...), custom_call_target="tpu_custom_call" | custom-call | tf_op jit(solution)/shard_map/pallas_call | solution.py:424
  20.6 0.0 collective-permute-done.3.beside_ref
  20.6 0.9 %shard_map.53 = (bf16[3,256,128]{2,1,0:T(8,128)(2,1)S(1)}, bf16[3,256,128]{2,1,0:T(8,128)(2,1)S(1)}, f32[32,256]{1,0:T(8,128)S(1)}) custom-call(s32[1]{0:T(128)S(6)} %copy.7.flag_ref.refs_0_, bf16[3,32,4,16,128]{4,3,2,1,0:T(8,128)(2,1)S(1)} %copy-done.1, f32[3,4,16,128]{3,2,1,0:T(8,128)S(1)} %copy-done.2, ...), custom_call_target="tpu_custom_call" | custom-call | tf_op jit(solution)/shard_map/pallas_call | solution.py:437
  21.5 0.0 collective-permute-done.2.refs_4_
  21.5 1.3 %shard_map.54 = (bf16[3,256,128]{2,1,0:T(8,128)(2,1)S(1)}, bf16[3,256,128]{2,1,0:T(8,128)(2,1)S(1)}, f32[16,1,640]{2,1,0:T(1,128)S(1)}) custom-call(s32[1]{0:T(128)S(6)} %copy.7.flag_ref.refs_0_, bf16[3,32,4,16,128]{4,3,2,1,0:T(8,128)(2,1)S(1)} %copy-done.1, f32[3,4,16,128]{3,2,1,0:T(8,128)S(1)} %copy-done.2, ...), custom_call_target="tpu_custom_call" | custom-call | tf_op jit(solution)/shard_map/pallas_call | solution.py:445
  22.8 16.7 %all_to_all.10 = f32[16,1,640]{2,1,0:T(1,128)S(1)} all-to-all(f32[16,1,640]{2,1,0:T(1,128)S(1)} %get-tuple-element.25), channel_id=1, replica_groups=mesh['blk'=32,'gz'=16] {'gz'}, dimensions={0} | all-to-all | bytes 81920 | tf_op jit(solution)/shard_map/all_to_all | solution.py:454
  39.7 17.9 %all_to_all.11 = f32[32,1,640]{2,1,0:T(1,128)S(1)} all-to-all(f32[32,1,640]{2,1,0:T(1,128)S(1)} %broadcast_in_dim.2), channel_id=1, replica_groups=mesh['blk'=32,'gz'=16] {'blk'}, dimensions={0} | all-to-all | bytes 163840 | tf_op jit(solution)/shard_map/all_to_all | solution.py:456
  57.6 0.1 reduce_sum.21
  57.7 3.3 %shard_map.55 = (f32[4,16,4,16,128]{4,3,2,1,0:T(8,128)}, f32[32,32]{1,0:T(8,128)}) custom-call(f32[1,640]{1,0:T(1,128)S(1)} %reduce_sum.22.sum_ref, bf16[4,2,256,128]{3,2,1,0:T(8,128)(2,1)S(1)} %get-tuple-element.26.xhi_ref, bf16[4,2,256,128]{3,2,1,0:T(8,128)(2,1)S(1)} %get-tuple-element.27.xli_ref, bf16[2,256,128]{2,1,0:T(8,128)(2,1)S(1)} %get-tuple-element.28.xhs_ref, ...), custom_call_target="tpu_custom_call" | custom-call | tf_op jit(solution)/shard_map/pallas_call | solution.py:458
  (3 shorter events, 0.1 us)
Async XLA Ops:
  1.3 1.4 %copy-start = (bf16[3,32,4,16,128]{4,3,2,1,0:T(8,128)(2,1)S(1)}, bf16[3,32,4,16,128]{4,3,2,1,0:T(8,128)(2,1)}, u32[]{:S(2)}) copy-start(bf16[3,32,4,16,128]{4,3,2,1,0:T(8,128)(2,1)} %refs_1_.1) | copy-start | bytes 4718596
  2.7 15.1 %copy-start.1 = (bf16[3,32,4,16,128]{4,3,2,1,0:T(8,128)(2,1)S(1)}, bf16[3,32,4,16,128]{4,3,2,1,0:T(8,128)(2,1)}, u32[]{:S(2)}) copy-start(bf16[3,32,4,16,128]{4,3,2,1,0:T(8,128)(2,1)} %refs_1_.1) | copy-start | bytes 4718596
  2.7 15.1 %copy-start.2 = (f32[3,4,16,128]{3,2,1,0:T(8,128)S(1)}, f32[3,4,16,128]{3,2,1,0:T(8,128)}, u32[]{:S(2)}) copy-start(f32[3,4,16,128]{3,2,1,0:T(8,128)} %refs_2_.1) | copy-start | bytes 294916
  3.2 17.4 %collective-permute-start.3 = (bf16[3,32,16,128]{3,2,1,0:T(8,128)(2,1)S(1)}, bf16[3,32,16,128]{3,2,1,0:T(8,128)(2,1)S(1)}, u32[]{:S(2)}, u32[]{:S(2)}) collective-permute-start(bf16[3,32,16,128]{3,2,1,0:T(8,128)(2,1)S(1)} %get-tuple-element.22), channel_id=1, source_target_pairs={{16,32},{48,64},{80,96},{112,128},{144,160},{176,192},{208,224},{2... | collective-permute-start | bytes 1179656 | tf_op jit(solution)/shard_map/ppermute | solution.py:407
  3.9 17.6 %collective-permute-start.2 = (bf16[3,32,16,128]{3,2,1,0:T(8,128)(2,1)S(1)}, bf16[3,32,16,128]{3,2,1,0:T(8,128)(2,1)S(1)}, u32[]{:S(2)}, u32[]{:S(2)}) collective-permute-start(bf16[3,32,16,128]{3,2,1,0:T(8,128)(2,1)S(1)} %get-tuple-element.21), channel_id=1, source_target_pairs={{0,16},{32,48},{64,80},{96,112},{128,144},{160,176},{192,208},{224... | collective-permute-start | bytes 1179656 | tf_op jit(solution)/shard_map/ppermute | solution.py:409
  10.9 4.2 %collective-permute-start = (bf16[128,128]{1,0:T(8,128)(2,1)S(1)}, bf16[128,128]{1,0:T(8,128)(2,1)S(1)}, u32[]{:S(2)}, u32[]{:S(2)}) collective-permute-start(bf16[128,128]{1,0:T(8,128)(2,1)S(1)} %get-tuple-element.18), channel_id=1, source_target_pairs={{0,1},{1,2},{2,3},{3,4},{4,5},{5,6},{6,7},{7,8},{8,9},{9,10},{10,1... | collective-permute-start | bytes 98312 | tf_op jit(solution)/shard_map/ppermute | solution.py:419
  14.1 3.6 %collective-permute-start.1 = (bf16[128,128]{1,0:T(8,128)(2,1)S(1)}, bf16[128,128]{1,0:T(8,128)(2,1)S(1)}, u32[]{:S(2)}, u32[]{:S(2)}) collective-permute-start(bf16[128,128]{1,0:T(8,128)(2,1)S(1)} %get-tuple-element.19), channel_id=1, source_target_pairs={{1,0},{2,1},{3,2},{4,3},{5,4},{6,5},{7,6},{8,7},{9,8},{10,9},{11,1... | collective-permute-start | bytes 98312 | tf_op jit(solution)/shard_map/ppermute | solution.py:420

commit v4 on v3

--- a/solution.py
+++ b/solution.py
@@ -185,10 +185,14 @@
     gram_ref[...] = folded_gram(hi, lo)
 
 
-def outer_plane(far, flag_ref, vel_ref, met_ref, side_ref, beside_ref, xh_ref, xl_ref, hi, lo):
+def outer_plane(
+    far, flag_ref, vel_ref, met_ref, xhs_ref, xls_ref, side_ref, beside_ref, xh_ref, xl_ref, hi, lo
+):
     even = 1 - (lax.axis_index("blk") & 1)
     is_first = even if not far else 1 - even
     x, place = 3 - 3 * is_first, 1 - is_first
+    xh_ref[0] = xhs_ref[place]
+    xl_ref[0] = xls_ref[place]
     flag = flag_ref[0] * is_first
     flip = flip_matrix(128, flag).astype(F32)
     sign = jnp.where(is_first == 1, -1.0, 1.0).astype(F32)
@@ -214,23 +218,27 @@
         gy0, gz0 = side_ref[place, 0, snaps], side_ref[place, 1, snaps]
         q_value = side_ref[place, 2, snaps] - 0.5 * (gx[0] * gx[0]) - (gy0 * gx[1] + gz0 * gx[2])
         for feature, value in enumerate((gz0 - gx[2], gx[1] - gy0, q_value)):
-            store_feature(value * weight, part, feature, xh_ref, xl_ref, (feature,), hi, lo)
+            store_feature(value * weight, part, feature, xh_ref, xl_ref, (feature + 1,), hi, lo)
     return folded_gram(hi, lo)
 
 
 def near_kernel(
-    flag_ref, vel_ref, met_ref, side_ref, beside_ref, before_ref, xh_ref, xl_ref, gram_ref, hi, lo
+    flag_ref, vel_ref, met_ref, xhs_ref, xls_ref, side_ref, beside_ref, before_ref,
+    xh_ref, xl_ref, gram_ref, hi, lo,
 ):
     gram_ref[...] = before_ref[...] + outer_plane(
-        False, flag_ref, vel_ref, met_ref, side_ref, beside_ref, xh_ref, xl_ref, hi, lo
+        False, flag_ref, vel_ref, met_ref, xhs_ref, xls_ref, side_ref, beside_ref,
+        xh_ref, xl_ref, hi, lo,
     )
 
 
 def far_kernel(
-    cells, flag_ref, vel_ref, met_ref, side_ref, beside_ref, before_ref, xh_ref, xl_ref, sent_ref, hi, lo
+    cells, flag_ref, vel_ref, met_ref, xhs_ref, xls_ref, side_ref, beside_ref, before_ref,
+    xh_ref, xl_ref, sent_ref, hi, lo,
 ):
     part = before_ref[...] + outer_plane(
-        True, flag_ref, vel_ref, met_ref, side_ref, beside_ref, xh_ref, xl_ref, hi, lo
+        True, flag_ref, vel_ref, met_ref, xhs_ref, xls_ref, side_ref, beside_ref,
+        xh_ref, xl_ref, hi, lo,
     )
     part = part * (0.5 / (4.0 * cells))
     row, col = iota((32, 256), 0), iota((32, 256), 1)
@@ -313,7 +321,7 @@
 
 
 def final_kernel(
-    sum_ref, xhi_ref, xli_ref, xhs_ref, xls_ref, xhn_ref, xln_ref, xhf_ref, xlf_ref,
+    sum_ref, xhi_ref, xli_ref, xhn_ref, xln_ref, xhf_ref, xlf_ref,
     modes_ref, r_ref, wide, out, sem,
 ):
     even = 1 - (lax.axis_index("blk") & 1)
@@ -348,34 +356,30 @@
     high, low = split(spread)
     wide[:256] = high
     wide[256:] = low
-    copies = []
+    def copy_out(feature):
+        return pltpu.make_async_copy(out.at[feature], modes_ref.at[feature], sem.at[feature])
+
     for feature in range(4):
-        if feature == 0:
-            places = (0, 1, 2, 3)
-            pieces = [(xhs_ref[0], xls_ref[0]), (xhs_ref[1], xls_ref[1])]
-        else:
-            places = (3 - 3 * even, 1, 2, 3 * even)
-            pieces = [
-                (xhn_ref[feature - 1], xln_ref[feature - 1]),
-                (xhf_ref[feature - 1], xlf_ref[feature - 1]),
-            ]
-        for place in (1, 0):
-            pieces.insert(1, (xhi_ref[feature, place], xli_ref[feature, place]))
-        highs = jnp.concatenate([piece[0] for piece in pieces], axis=1)
-        lows = jnp.concatenate([piece[1] for piece in pieces], axis=1)
+        pieces = (
+            (xhn_ref, xln_ref, (feature,), 3 - 3 * even),
+            (xhi_ref, xli_ref, (feature, 0), 1),
+            (xhi_ref, xli_ref, (feature, 1), 2),
+            (xhf_ref, xlf_ref, (feature,), 3 * even),
+        )
+        highs = jnp.concatenate([piece[0][piece[2]] for piece in pieces], axis=1)
+        lows = jnp.concatenate([piece[1][piece[2]] for piece in pieces], axis=1)
         both = dot(wide[...], highs)
         modes = both[:256] + both[256:] + dot(wide[:256], lows)
-        for n, x in enumerate(places):
-            out[feature, :, x] = modes[:, 128 * n : 128 * n + 128].reshape(16, 16, 128)
-        gram, _ = eliminate(KEEP + 4 * feature, gram, [])
-        copy = pltpu.make_async_copy(out.at[feature], modes_ref.at[feature], sem.at[feature])
-        copy.start()
-        copies.append(copy)
+        for n, piece in enumerate(pieces):
+            out[feature, :, piece[3]] = modes[:, 128 * n : 128 * n + 128].reshape(16, 16, 128)
+        copy_out(feature).start()
+    for first in range(KEEP, 32, 4):
+        gram, _ = eliminate(first, gram, [])
     row, col = iota((32, 32), 0), iota((32, 32), 1)
     whole = jnp.concatenate(gram, axis=0)[:, :32]
     r_ref[...] = jnp.where(col >= row, whole, 0.0)
-    for copy in copies:
-        copy.wait()
+    for feature in range(4):
+        copy_out(feature).wait()
 
 
 def vmem():
@@ -419,7 +423,7 @@
     low = lax.ppermute(last, "gz", [(i, (i + 1) % n_gz) for i in range(n_gz)])
     high = lax.ppermute(first, "gz", [((i + 1) % n_gz, i) for i in range(n_gz)])
 
-    half, outer, side = shape((4, 2, 256, 128), BF), shape((3, 256, 128), BF), shape((2, 256, 128), BF)
+    half, outer, side = shape((4, 2, 256, 128), BF), shape((4, 256, 128), BF), shape((2, 256, 128), BF)
     folded = shape((32, 256), F32)
     xhi, xli, xhs, xls, sides, gram = pl.pallas_call(
         inner_kernel,
@@ -437,19 +441,19 @@
     xhn, xln, gram = pl.pallas_call(
         near_kernel,
         out_shape=(outer, outer, folded),
-        in_specs=[smem()] + [vmem()] * 5,
+        in_specs=[smem()] + [vmem()] * 7,
         out_specs=(vmem(),) * 3,
         scratch_shapes=scratch,
         compiler_params=params(24),
-    )(face_flip, velocity, metric, sides, near_in, gram)
+    )(face_flip, velocity, metric, xhs, xls, sides, near_in, gram)
     xhf, xlf, sent = pl.pallas_call(
         far_plane,
         out_shape=(outer, outer, shape((n_gz, 1, 640), F32)),
-        in_specs=[smem()] + [vmem()] * 5,
+        in_specs=[smem()] + [vmem()] * 7,
         out_specs=(vmem(),) * 3,
         scratch_shapes=scratch,
         compiler_params=params(24),
-    )(face_flip, velocity, metric, sides, far_in, gram)
+    )(face_flip, velocity, metric, xhs, xls, sides, far_in, gram)
 
     part = jnp.sum(lax.all_to_all(sent, "gz", 0, 0), axis=0)
     part = jnp.broadcast_to(part[None], (n_blk, 1, 640))
@@ -458,7 +462,7 @@
     modes, r_factor = pl.pallas_call(
         final_kernel,
         out_shape=(shape((4, 16, 4, 16, 128), F32), shape((32, 32), F32)),
-        in_specs=[vmem()] * 9,
+        in_specs=[vmem()] * 7,
         out_specs=(pl.BlockSpec(memory_space=pltpu.HBM), vmem()),
         scratch_shapes=[
             pltpu.VMEM((512, 256), BF),
@@ -466,7 +470,7 @@
             pltpu.SemaphoreType.DMA((4,)),
         ],
         compiler_params=params(24),
-    )(whole, xhi, xli, xhs, xls, xhn, xln, xhf, xlf)
+    )(whole, xhi, xli, xhn, xln, xhf, xlf)
     return (modes, r_factor)
 
 

time: 61.3 us -> 61.3 us (level)
  no operation moved by 1% of the time
where the time goes in v4:
time: 61.3 us; the launch traced here: 61 us
  blocking collectives  34.7 us (57%)
  starting transfers between devices  10.6 us (17%)
  Pallas kernels  9.14 us (15%)
  waiting for transfers between devices  3.64 us (6%)
  local copies, waits for them, and re-layouts  1.46 us (2%)
  between operations  1.37 us (2%)
    all_to_all x1, blocking collectives, local(): whole = jnp.sum(lax.all_to_all(part, 'blk', 0, 0), axis=0)  17.9 us
    all_to_all x1, blocking collectives, local(): part = jnp.sum(lax.all_to_all(sent, 'gz', 0, 0), axis=0)  16.7 us
    ppermute x1, starting transfers between devices, local(): far_in = lax.ppermute(far_out, 'blk', pairs + [(b, a) for a, b in pairs])  6.6 us
    pallas_call x1, Pallas kernels, local(): pl.pallas_call(final_kernel, out_shape=(shape((4, 16, 4, 16, 128), F32),...  3.35 us
    ppermute x1, starting transfers between devices, local(): low = lax.ppermute(last, 'gz', [(i, (i + 1) % n_gz) for i in range(n_gz)])  3.23 us
    pallas_call x1, Pallas kernels, local(): pl.pallas_call(inner_kernel, out_shape=(half, half, side, side, shape((2,...  2.85 us
    ppermute x1, waiting for transfers between devices, local(): high = lax.ppermute(first, 'gz', [((i + 1) % n_gz, i) for i in range(n_gz)])  2.61 us
    unnamed x6, local copies, waits for them, and re-layouts  1.41 us
  transfers between devices with their start and end apart: 4, of which 2 were waited for; matrix products, arithmetic and copies ran while one was open for 0% of the time, Pallas kernels for 7%

profile of v4, /device:TPU:1, one launch (start us, length us, event | category | flops | bytes accessed | tf_op | source)
XLA Modules:
  0.0 61.0 jit_solution(17325315696462215391)
XLA Ops:
  1.3 0.0 copy-start
  1.3 1.4 %copy-done = bf16[3,32,4,16,128]{4,3,2,1,0:T(8,128)(2,1)S(1)} copy-done((bf16[3,32,4,16,128]{4,3,2,1,0:T(8,128)(2,1)S(1)}, bf16[3,32,4,16,128]{4,3,2,1,0:T(8,128)(2,1)}, u32[]{:S(2)}) %copy-start) | copy-done | bytes 1572888
  2.7 0.0 copy-start.1
  2.7 0.0 copy-start.2
  2.7 0.2 shard_map.52
  2.9 0.8 %collective-permute-start.3 = (bf16[3,32,16,128]{3,2,1,0:T(8,128)(2,1)S(1)}, bf16[3,32,16,128]{3,2,1,0:T(8,128)(2,1)S(1)}, u32[]{:S(2)}, u32[]{:S(2)}) collective-permute-start(bf16[3,32,16,128]{3,2,1,0:T(8,128)(2,1)S(1)} %get-tuple-element.24), channel_id=1, source_target_pairs={{16,32},{48,64},{80,96},{112,128},{144,160},{176,192},{208,224},{2... | collective-permute-start | bytes 1179656 | tf_op jit(solution)/shard_map/ppermute | solution.py:411
  3.7 6.6 %collective-permute-start.2 = (bf16[3,32,16,128]{3,2,1,0:T(8,128)(2,1)S(1)}, bf16[3,32,16,128]{3,2,1,0:T(8,128)(2,1)S(1)}, u32[]{:S(2)}, u32[]{:S(2)}) collective-permute-start(bf16[3,32,16,128]{3,2,1,0:T(8,128)(2,1)S(1)} %get-tuple-element.23), channel_id=1, source_target_pairs={{0,16},{32,48},{64,80},{96,112},{128,144},{160,176},{192,208},{224... | collective-permute-start | bytes 1179656 | tf_op jit(solution)/shard_map/ppermute | solution.py:413
  10.3 0.6 shard_map.50
  10.9 3.2 %collective-permute-start = (bf16[128,128]{1,0:T(8,128)(2,1)S(1)}, bf16[128,128]{1,0:T(8,128)(2,1)S(1)}, u32[]{:S(2)}, u32[]{:S(2)}) collective-permute-start(bf16[128,128]{1,0:T(8,128)(2,1)S(1)} %get-tuple-element.18), channel_id=1, source_target_pairs={{0,1},{1,2},{2,3},{3,4},{4,5},{5,6},{6,7},{7,8},{8,9},{9,10},{10,1... | collective-permute-start | bytes 98312 | tf_op jit(solution)/shard_map/ppermute | solution.py:423
  14.1 0.0 collective-permute-start.1
  14.1 1.0 %collective-permute-done.low_ref = bf16[128,128]{1,0:T(8,128)(2,1)S(1)} collective-permute-done((bf16[128,128]{1,0:T(8,128)(2,1)S(1)}, bf16[128,128]{1,0:T(8,128)(2,1)S(1)}, u32[]{:S(2)}, u32[]{:S(2)}) %collective-permute-start) | collective-permute-done | bytes 32800 | tf_op jit(solution)/shard_map/ppermute | solution.py:423
  15.1 2.6 %collective-permute-done.1.high_ref = bf16[128,128]{1,0:T(8,128)(2,1)S(1)} collective-permute-done((bf16[128,128]{1,0:T(8,128)(2,1)S(1)}, bf16[128,128]{1,0:T(8,128)(2,1)S(1)}, u32[]{:S(2)}, u32[]{:S(2)}) %collective-permute-start.1) | collective-permute-done | bytes 32800 | tf_op jit(solution)/shard_map/ppermute | solution.py:424
  17.7 0.0 copy-done.1
  17.7 0.0 copy-done.2
  17.7 2.9 %shard_map.51 = (bf16[4,2,256,128]{3,2,1,0:T(8,128)(2,1)S(1)}, bf16[4,2,256,128]{3,2,1,0:T(8,128)(2,1)S(1)}, bf16[2,256,128]{2,1,0:T(8,128)(2,1)S(1)}, bf16[2,25...) custom-call(bf16[3,32,4,16,128]{4,3,2,1,0:T(8,128)(2,1)S(1)} %copy-done.1, ...), custom_call_target="tpu_custom_call" | custom-call | tf_op jit(solution)/shard_map/pallas_call | solution.py:428
  20.6 0.0 collective-permute-done.3.beside_ref
  20.6 0.9 %shard_map.53 = (bf16[4,256,128]{2,1,0:T(8,128)(2,1)S(1)}, bf16[4,256,128]{2,1,0:T(8,128)(2,1)S(1)}, f32[32,256]{1,0:T(8,128)S(1)}) custom-call(s32[1]{0:T(128)S(6)} %copy.7.flag_ref.refs_0_, bf16[3,32,4,16,128]{4,3,2,1,0:T(8,128)(2,1)S(1)} %copy-done.1, f32[3,4,16,128]{3,2,1,0:T(8,128)S(1)} %copy-done.2, ...), custom_call_target="tpu_custom_call" | custom-call | tf_op jit(solution)/shard_map/pallas_call | solution.py:441
  21.5 0.0 collective-permute-done.2.refs_6_
  21.6 1.3 %shard_map.54 = (bf16[4,256,128]{2,1,0:T(8,128)(2,1)S(1)}, bf16[4,256,128]{2,1,0:T(8,128)(2,1)S(1)}, f32[16,1,640]{2,1,0:T(1,128)S(1)}) custom-call(s32[1]{0:T(128)S(6)} %copy.7.flag_ref.refs_0_, bf16[3,32,4,16,128]{4,3,2,1,0:T(8,128)(2,1)S(1)} %copy-done.1, f32[3,4,16,128]{3,2,1,0:T(8,128)S(1)} %copy-done.2, ...), custom_call_target="tpu_custom_call" | custom-call | tf_op jit(solution)/shard_map/pallas_call | solution.py:449
  22.8 16.7 %all_to_all.10 = f32[16,1,640]{2,1,0:T(1,128)S(1)} all-to-all(f32[16,1,640]{2,1,0:T(1,128)S(1)} %get-tuple-element.27), channel_id=1, replica_groups=mesh['blk'=32,'gz'=16] {'gz'}, dimensions={0} | all-to-all | bytes 81920 | tf_op jit(solution)/shard_map/all_to_all | solution.py:458
  39.7 17.9 %all_to_all.11 = f32[32,1,640]{2,1,0:T(1,128)S(1)} all-to-all(f32[32,1,640]{2,1,0:T(1,128)S(1)} %broadcast_in_dim.2), channel_id=1, replica_groups=mesh['blk'=32,'gz'=16] {'blk'}, dimensions={0} | all-to-all | bytes 163840 | tf_op jit(solution)/shard_map/all_to_all | solution.py:460
  57.6 0.1 reduce_sum.21
  57.7 3.3 %shard_map.55 = (f32[4,16,4,16,128]{4,3,2,1,0:T(8,128)}, f32[32,32]{1,0:T(8,128)}) custom-call(f32[1,640]{1,0:T(1,128)S(1)} %reduce_sum.22.sum_ref, bf16[4,2,256,128]{3,2,1,0:T(8,128)(2,1)S(1)} %get-tuple-element.28.xhi_ref, bf16[4,2,256,128]{3,2,1,0:T(8,128)(2,1)S(1)} %get-tuple-element.29.xli_ref, bf16[4,256,128]{2,1,0:T(8,128)(2,1)S(1)} %get-tuple-element.30.xhn_ref, ...), custom_call_target="tpu_custom_call" | custom-call | tf_op jit(solution)/shard_map/pallas_call | solution.py:462
  (3 shorter events, 0.1 us)
Async XLA Ops:
  1.3 1.4 %copy-start = (bf16[3,32,4,16,128]{4,3,2,1,0:T(8,128)(2,1)S(1)}, bf16[3,32,4,16,128]{4,3,2,1,0:T(8,128)(2,1)}, u32[]{:S(2)}) copy-start(bf16[3,32,4,16,128]{4,3,2,1,0:T(8,128)(2,1)} %refs_1_.1) | copy-start | bytes 4718596
  2.7 15.1 %copy-start.1 = (bf16[3,32,4,16,128]{4,3,2,1,0:T(8,128)(2,1)S(1)}, bf16[3,32,4,16,128]{4,3,2,1,0:T(8,128)(2,1)}, u32[]{:S(2)}) copy-start(bf16[3,32,4,16,128]{4,3,2,1,0:T(8,128)(2,1)} %refs_1_.1) | copy-start | bytes 4718596
  2.7 15.1 %copy-start.2 = (f32[3,4,16,128]{3,2,1,0:T(8,128)S(1)}, f32[3,4,16,128]{3,2,1,0:T(8,128)}, u32[]{:S(2)}) copy-start(f32[3,4,16,128]{3,2,1,0:T(8,128)} %refs_2_.1) | copy-start | bytes 294916
  2.9 17.7 %collective-permute-start.3 = (bf16[3,32,16,128]{3,2,1,0:T(8,128)(2,1)S(1)}, bf16[3,32,16,128]{3,2,1,0:T(8,128)(2,1)S(1)}, u32[]{:S(2)}, u32[]{:S(2)}) collective-permute-start(bf16[3,32,16,128]{3,2,1,0:T(8,128)(2,1)S(1)} %get-tuple-element.24), channel_id=1, source_target_pairs={{16,32},{48,64},{80,96},{112,128},{144,160},{176,192},{208,224},{2... | collective-permute-start | bytes 1179656 | tf_op jit(solution)/shard_map/ppermute | solution.py:411
  3.7 17.9 %collective-permute-start.2 = (bf16[3,32,16,128]{3,2,1,0:T(8,128)(2,1)S(1)}, bf16[3,32,16,128]{3,2,1,0:T(8,128)(2,1)S(1)}, u32[]{:S(2)}, u32[]{:S(2)}) collective-permute-start(bf16[3,32,16,128]{3,2,1,0:T(8,128)(2,1)S(1)} %get-tuple-element.23), channel_id=1, source_target_pairs={{0,16},{32,48},{64,80},{96,112},{128,144},{160,176},{192,208},{224... | collective-permute-start | bytes 1179656 | tf_op jit(solution)/shard_map/ppermute | solution.py:413
  10.9 4.2 %collective-permute-start = (bf16[128,128]{1,0:T(8,128)(2,1)S(1)}, bf16[128,128]{1,0:T(8,128)(2,1)S(1)}, u32[]{:S(2)}, u32[]{:S(2)}) collective-permute-start(bf16[128,128]{1,0:T(8,128)(2,1)S(1)} %get-tuple-element.18), channel_id=1, source_target_pairs={{0,1},{1,2},{2,3},{3,4},{4,5},{5,6},{6,7},{7,8},{8,9},{9,10},{10,1... | collective-permute-start | bytes 98312 | tf_op jit(solution)/shard_map/ppermute | solution.py:423
  14.1 3.6 %collective-permute-start.1 = (bf16[128,128]{1,0:T(8,128)(2,1)S(1)}, bf16[128,128]{1,0:T(8,128)(2,1)S(1)}, u32[]{:S(2)}, u32[]{:S(2)}) collective-permute-start(bf16[128,128]{1,0:T(8,128)(2,1)S(1)} %get-tuple-element.19), channel_id=1, source_target_pairs={{1,0},{2,1},{3,2},{4,3},{5,4},{6,5},{7,6},{8,7},{9,8},{10,9},{11,1... | collective-permute-start | bytes 98312 | tf_op jit(solution)/shard_map/ppermute | solution.py:424

commit v5 on v4

--- a/solution.py
+++ b/solution.py
@@ -359,7 +359,7 @@
     def copy_out(feature):
         return pltpu.make_async_copy(out.at[feature], modes_ref.at[feature], sem.at[feature])
 
-    for feature in range(4):
+    def one_feature(feature, carry):
         pieces = (
             (xhn_ref, xln_ref, (feature,), 3 - 3 * even),
             (xhi_ref, xli_ref, (feature, 0), 1),
@@ -373,6 +373,9 @@
         for n, piece in enumerate(pieces):
             out[feature, :, piece[3]] = modes[:, 128 * n : 128 * n + 128].reshape(16, 16, 128)
         copy_out(feature).start()
+        return carry
+
+    lax.fori_loop(0, 4, one_feature, 0)
     for first in range(KEEP, 32, 4):
         gram, _ = eliminate(first, gram, [])
     row, col = iota((32, 32), 0), iota((32, 32), 1)

time: 61.3 us -> 61.9 us (level)
  Pallas kernels: 9.14 us -> 10.1 us
    pallas_call x1, Pallas kernels: 3.35 us -> 3.99 us  [local(): pl.pallas_call(final_kernel, out_shape=(shape((4, 16, 4, 16, 128), F32),...]
where the time goes in v5:
time: 61.9 us; the launch traced here: 61.7 us
  blocking collectives  34.7 us (56%)
  starting transfers between devices  10.3 us (17%)
  Pallas kernels  10.1 us (16%)
  waiting for transfers between devices  3.64 us (6%)
  local copies, waits for them, and re-layouts  1.46 us (2%)
  between operations  1.37 us (2%)
    all_to_all x1, blocking collectives, local(): whole = jnp.sum(lax.all_to_all(part, 'blk', 0, 0), axis=0)  17.9 us
    all_to_all x1, blocking collectives, local(): part = jnp.sum(lax.all_to_all(sent, 'gz', 0, 0), axis=0)  16.7 us
    ppermute x1, starting transfers between devices, local(): far_in = lax.ppermute(far_out, 'blk', pairs + [(b, a) for a, b in pairs])  6.38 us
    pallas_call x1, Pallas kernels, local(): pl.pallas_call(final_kernel, out_shape=(shape((4, 16, 4, 16, 128), F32),...  3.99 us
    ppermute x1, starting transfers between devices, local(): low = lax.ppermute(last, 'gz', [(i, (i + 1) % n_gz) for i in range(n_gz)])  3.23 us
    pallas_call x1, Pallas kernels, local(): pl.pallas_call(inner_kernel, out_shape=(half, half, side, side, shape((2,...  2.85 us
    ppermute x1, waiting for transfers between devices, local(): high = lax.ppermute(first, 'gz', [((i + 1) % n_gz, i) for i in range(n_gz)])  2.61 us
    unnamed x6, local copies, waits for them, and re-layouts  1.41 us
  transfers between devices with their start and end apart: 4, of which 2 were waited for; matrix products, arithmetic and copies ran while one was open for 0% of the time, Pallas kernels for 7%

profile of v5, /device:TPU:1, one launch (start us, length us, event | category | flops | bytes accessed | tf_op | source)
XLA Modules:
  0.0 61.7 jit_solution(17730374213505456691)
XLA Ops:
  1.3 0.0 copy-start
  1.3 1.4 %copy-done = bf16[3,32,4,16,128]{4,3,2,1,0:T(8,128)(2,1)S(1)} copy-done((bf16[3,32,4,16,128]{4,3,2,1,0:T(8,128)(2,1)S(1)}, bf16[3,32,4,16,128]{4,3,2,1,0:T(8,128)(2,1)}, u32[]{:S(2)}) %copy-start) | copy-done | bytes 1572888
  2.7 0.0 copy-start.1
  2.7 0.0 copy-start.2
  2.7 0.5 shard_map.52
  3.2 0.7 %collective-permute-start.3 = (bf16[3,32,16,128]{3,2,1,0:T(8,128)(2,1)S(1)}, bf16[3,32,16,128]{3,2,1,0:T(8,128)(2,1)S(1)}, u32[]{:S(2)}, u32[]{:S(2)}) collective-permute-start(bf16[3,32,16,128]{3,2,1,0:T(8,128)(2,1)S(1)} %get-tuple-element.24), channel_id=1, source_target_pairs={{16,32},{48,64},{80,96},{112,128},{144,160},{176,192},{208,224},{2... | collective-permute-start | bytes 1179656 | tf_op jit(solution)/shard_map/ppermute | solution.py:414
  3.9 6.4 %collective-permute-start.2 = (bf16[3,32,16,128]{3,2,1,0:T(8,128)(2,1)S(1)}, bf16[3,32,16,128]{3,2,1,0:T(8,128)(2,1)S(1)}, u32[]{:S(2)}, u32[]{:S(2)}) collective-permute-start(bf16[3,32,16,128]{3,2,1,0:T(8,128)(2,1)S(1)} %get-tuple-element.23), channel_id=1, source_target_pairs={{0,16},{32,48},{64,80},{96,112},{128,144},{160,176},{192,208},{224... | collective-permute-start | bytes 1179656 | tf_op jit(solution)/shard_map/ppermute | solution.py:416
  10.3 0.6 shard_map.50
  10.9 3.2 %collective-permute-start = (bf16[128,128]{1,0:T(8,128)(2,1)S(1)}, bf16[128,128]{1,0:T(8,128)(2,1)S(1)}, u32[]{:S(2)}, u32[]{:S(2)}) collective-permute-start(bf16[128,128]{1,0:T(8,128)(2,1)S(1)} %get-tuple-element.18), channel_id=1, source_target_pairs={{0,1},{1,2},{2,3},{3,4},{4,5},{5,6},{6,7},{7,8},{8,9},{9,10},{10,1... | collective-permute-start | bytes 98312 | tf_op jit(solution)/shard_map/ppermute | solution.py:426
  14.1 0.0 collective-permute-start.1
  14.1 1.0 %collective-permute-done.low_ref = bf16[128,128]{1,0:T(8,128)(2,1)S(1)} collective-permute-done((bf16[128,128]{1,0:T(8,128)(2,1)S(1)}, bf16[128,128]{1,0:T(8,128)(2,1)S(1)}, u32[]{:S(2)}, u32[]{:S(2)}) %collective-permute-start) | collective-permute-done | bytes 32800 | tf_op jit(solution)/shard_map/ppermute | solution.py:426
  15.1 2.6 %collective-permute-done.1.high_ref = bf16[128,128]{1,0:T(8,128)(2,1)S(1)} collective-permute-done((bf16[128,128]{1,0:T(8,128)(2,1)S(1)}, bf16[128,128]{1,0:T(8,128)(2,1)S(1)}, u32[]{:S(2)}, u32[]{:S(2)}) %collective-permute-start.1) | collective-permute-done | bytes 32800 | tf_op jit(solution)/shard_map/ppermute | solution.py:427
  17.7 0.0 copy-done.1
  17.7 0.0 copy-done.2
  17.7 2.9 %shard_map.51 = (bf16[4,2,256,128]{3,2,1,0:T(8,128)(2,1)S(1)}, bf16[4,2,256,128]{3,2,1,0:T(8,128)(2,1)S(1)}, bf16[2,256,128]{2,1,0:T(8,128)(2,1)S(1)}, bf16[2,25...) custom-call(bf16[3,32,4,16,128]{4,3,2,1,0:T(8,128)(2,1)S(1)} %copy-done.1, ...), custom_call_target="tpu_custom_call" | custom-call | tf_op jit(solution)/shard_map/pallas_call | solution.py:431
  20.6 0.0 collective-permute-done.3.beside_ref
  20.6 0.9 %shard_map.53 = (bf16[4,256,128]{2,1,0:T(8,128)(2,1)S(1)}, bf16[4,256,128]{2,1,0:T(8,128)(2,1)S(1)}, f32[32,256]{1,0:T(8,128)S(1)}) custom-call(s32[1]{0:T(128)S(6)} %copy.7.flag_ref.refs_0_, bf16[3,32,4,16,128]{4,3,2,1,0:T(8,128)(2,1)S(1)} %copy-done.1, f32[3,4,16,128]{3,2,1,0:T(8,128)S(1)} %copy-done.2, ...), custom_call_target="tpu_custom_call" | custom-call | tf_op jit(solution)/shard_map/pallas_call | solution.py:444
  21.5 0.0 collective-permute-done.2.refs_6_
  21.6 1.3 %shard_map.54 = (bf16[4,256,128]{2,1,0:T(8,128)(2,1)S(1)}, bf16[4,256,128]{2,1,0:T(8,128)(2,1)S(1)}, f32[16,1,640]{2,1,0:T(1,128)S(1)}) custom-call(s32[1]{0:T(128)S(6)} %copy.7.flag_ref.refs_0_, bf16[3,32,4,16,128]{4,3,2,1,0:T(8,128)(2,1)S(1)} %copy-done.1, f32[3,4,16,128]{3,2,1,0:T(8,128)S(1)} %copy-done.2, ...), custom_call_target="tpu_custom_call" | custom-call | tf_op jit(solution)/shard_map/pallas_call | solution.py:452
  22.8 16.7 %all_to_all.10 = f32[16,1,640]{2,1,0:T(1,128)S(1)} all-to-all(f32[16,1,640]{2,1,0:T(1,128)S(1)} %get-tuple-element.27), channel_id=1, replica_groups=mesh['blk'=32,'gz'=16] {'gz'}, dimensions={0} | all-to-all | bytes 81920 | tf_op jit(solution)/shard_map/all_to_all | solution.py:461
  39.7 17.9 %all_to_all.11 = f32[32,1,640]{2,1,0:T(1,128)S(1)} all-to-all(f32[32,1,640]{2,1,0:T(1,128)S(1)} %broadcast_in_dim.2), channel_id=1, replica_groups=mesh['blk'=32,'gz'=16] {'blk'}, dimensions={0} | all-to-all | bytes 163840 | tf_op jit(solution)/shard_map/all_to_all | solution.py:463
  57.6 0.1 reduce_sum.21
  57.7 4.0 %shard_map.55 = (f32[4,16,4,16,128]{4,3,2,1,0:T(8,128)}, f32[32,32]{1,0:T(8,128)}) custom-call(f32[1,640]{1,0:T(1,128)S(1)} %reduce_sum.22.sum_ref, bf16[4,2,256,128]{3,2,1,0:T(8,128)(2,1)S(1)} %get-tuple-element.28.xhi_ref, bf16[4,2,256,128]{3,2,1,0:T(8,128)(2,1)S(1)} %get-tuple-element.29.xli_ref, bf16[4,256,128]{2,1,0:T(8,128)(2,1)S(1)} %get-tuple-element.30.xhn_ref, ...), custom_call_target="tpu_custom_call" | custom-call | tf_op jit(solution)/shard_map/pallas_call | solution.py:465
  (3 shorter events, 0.1 us)
Async XLA Ops:
  1.3 1.4 %copy-start = (bf16[3,32,4,16,128]{4,3,2,1,0:T(8,128)(2,1)S(1)}, bf16[3,32,4,16,128]{4,3,2,1,0:T(8,128)(2,1)}, u32[]{:S(2)}) copy-start(bf16[3,32,4,16,128]{4,3,2,1,0:T(8,128)(2,1)} %refs_1_.1) | copy-start | bytes 4718596
  2.7 15.1 %copy-start.1 = (bf16[3,32,4,16,128]{4,3,2,1,0:T(8,128)(2,1)S(1)}, bf16[3,32,4,16,128]{4,3,2,1,0:T(8,128)(2,1)}, u32[]{:S(2)}) copy-start(bf16[3,32,4,16,128]{4,3,2,1,0:T(8,128)(2,1)} %refs_1_.1) | copy-start | bytes 4718596
  2.7 15.1 %copy-start.2 = (f32[3,4,16,128]{3,2,1,0:T(8,128)S(1)}, f32[3,4,16,128]{3,2,1,0:T(8,128)}, u32[]{:S(2)}) copy-start(f32[3,4,16,128]{3,2,1,0:T(8,128)} %refs_2_.1) | copy-start | bytes 294916
  3.2 17.4 %collective-permute-start.3 = (bf16[3,32,16,128]{3,2,1,0:T(8,128)(2,1)S(1)}, bf16[3,32,16,128]{3,2,1,0:T(8,128)(2,1)S(1)}, u32[]{:S(2)}, u32[]{:S(2)}) collective-permute-start(bf16[3,32,16,128]{3,2,1,0:T(8,128)(2,1)S(1)} %get-tuple-element.24), channel_id=1, source_target_pairs={{16,32},{48,64},{80,96},{112,128},{144,160},{176,192},{208,224},{2... | collective-permute-start | bytes 1179656 | tf_op jit(solution)/shard_map/ppermute | solution.py:414
  3.9 17.6 %collective-permute-start.2 = (bf16[3,32,16,128]{3,2,1,0:T(8,128)(2,1)S(1)}, bf16[3,32,16,128]{3,2,1,0:T(8,128)(2,1)S(1)}, u32[]{:S(2)}, u32[]{:S(2)}) collective-permute-start(bf16[3,32,16,128]{3,2,1,0:T(8,128)(2,1)S(1)} %get-tuple-element.23), channel_id=1, source_target_pairs={{0,16},{32,48},{64,80},{96,112},{128,144},{160,176},{192,208},{224... | collective-permute-start | bytes 1179656 | tf_op jit(solution)/shard_map/ppermute | solution.py:416
  10.9 4.2 %collective-permute-start = (bf16[128,128]{1,0:T(8,128)(2,1)S(1)}, bf16[128,128]{1,0:T(8,128)(2,1)S(1)}, u32[]{:S(2)}, u32[]{:S(2)}) collective-permute-start(bf16[128,128]{1,0:T(8,128)(2,1)S(1)} %get-tuple-element.18), channel_id=1, source_target_pairs={{0,1},{1,2},{2,3},{3,4},{4,5},{5,6},{6,7},{7,8},{8,9},{9,10},{10,1... | collective-permute-start | bytes 98312 | tf_op jit(solution)/shard_map/ppermute | solution.py:426
  14.1 3.6 %collective-permute-start.1 = (bf16[128,128]{1,0:T(8,128)(2,1)S(1)}, bf16[128,128]{1,0:T(8,128)(2,1)S(1)}, u32[]{:S(2)}, u32[]{:S(2)}) collective-permute-start(bf16[128,128]{1,0:T(8,128)(2,1)S(1)} %get-tuple-element.19), channel_id=1, source_target_pairs={{1,0},{2,1},{3,2},{4,3},{5,4},{6,5},{7,6},{8,7},{9,8},{10,9},{11,1... | collective-permute-start | bytes 98312 | tf_op jit(solution)/shard_map/ppermute | solution.py:427

commit v6 on v4

--- a/solution.py
+++ b/solution.py
@@ -356,8 +356,11 @@
     high, low = split(spread)
     wide[:256] = high
     wide[256:] = low
-    def copy_out(feature):
-        return pltpu.make_async_copy(out.at[feature], modes_ref.at[feature], sem.at[feature])
+    def copy_out(feature, part):
+        place = (feature, pl.ds(8 * part, 8))
+        return pltpu.make_async_copy(
+            out.at[*place], modes_ref.at[*place], sem.at[2 * feature + part]
+        )
 
     for feature in range(4):
         pieces = (
@@ -368,18 +371,23 @@
         )
         highs = jnp.concatenate([piece[0][piece[2]] for piece in pieces], axis=1)
         lows = jnp.concatenate([piece[1][piece[2]] for piece in pieces], axis=1)
-        both = dot(wide[...], highs)
-        modes = both[:256] + both[256:] + dot(wide[:256], lows)
-        for n, piece in enumerate(pieces):
-            out[feature, :, piece[3]] = modes[:, 128 * n : 128 * n + 128].reshape(16, 16, 128)
-        copy_out(feature).start()
+        for part in range(2):
+            rows = slice(128 * part, 128 * part + 128)
+            modes = dot(wide[rows], highs) + dot(wide[rows], lows)
+            modes = modes + dot(wide[256 + 128 * part : 384 + 128 * part], highs)
+            for n, piece in enumerate(pieces):
+                out[feature, 8 * part : 8 * part + 8, piece[3]] = modes[
+                    :, 128 * n : 128 * n + 128
+                ].reshape(8, 16, 128)
+            copy_out(feature, part).start()
     for first in range(KEEP, 32, 4):
         gram, _ = eliminate(first, gram, [])
     row, col = iota((32, 32), 0), iota((32, 32), 1)
     whole = jnp.concatenate(gram, axis=0)[:, :32]
     r_ref[...] = jnp.where(col >= row, whole, 0.0)
     for feature in range(4):
-        copy_out(feature).wait()
+        copy_out(feature, 0).wait()
+        copy_out(feature, 1).wait()
 
 
 def vmem():
@@ -467,7 +475,7 @@
         scratch_shapes=[
             pltpu.VMEM((512, 256), BF),
             pltpu.VMEM((4, 16, 4, 16, 128), F32),
-            pltpu.SemaphoreType.DMA((4,)),
+            pltpu.SemaphoreType.DMA((8,)),
         ],
         compiler_params=params(24),
     )(whole, xhi, xli, xhn, xln, xhf, xlf)

time: 61.3 us -> 61.1 us (level)
  no operation moved by 1% of the time
where the time goes in v6:
time: 61.1 us; the launch traced here: 60.7 us
  blocking collectives  34.4 us (56%)
  starting transfers between devices  10.6 us (17%)
  Pallas kernels  9.08 us (15%)
  waiting for transfers between devices  3.64 us (6%)
  local copies, waits for them, and re-layouts  1.46 us (2%)
  between operations  1.37 us (2%)
    all_to_all x1, blocking collectives, local(): whole = jnp.sum(lax.all_to_all(part, 'blk', 0, 0), axis=0)  17.7 us
    all_to_all x1, blocking collectives, local(): part = jnp.sum(lax.all_to_all(sent, 'gz', 0, 0), axis=0)  16.7 us
    ppermute x1, starting transfers between devices, local(): far_in = lax.ppermute(far_out, 'blk', pairs + [(b, a) for a, b in pairs])  6.6 us
    pallas_call x1, Pallas kernels, local(): pl.pallas_call(final_kernel, out_shape=(shape((4, 16, 4, 16, 128), F32),...  3.29 us
    ppermute x1, starting transfers between devices, local(): low = lax.ppermute(last, 'gz', [(i, (i + 1) % n_gz) for i in range(n_gz)])  3.23 us
    pallas_call x1, Pallas kernels, local(): pl.pallas_call(inner_kernel, out_shape=(half, half, side, side, shape((2,...  2.85 us
    ppermute x1, waiting for transfers between devices, local(): high = lax.ppermute(first, 'gz', [((i + 1) % n_gz, i) for i in range(n_gz)])  2.61 us
    unnamed x6, local copies, waits for them, and re-layouts  1.41 us
  transfers between devices with their start and end apart: 4, of which 2 were waited for; matrix products, arithmetic and copies ran while one was open for 0% of the time, Pallas kernels for 7%

profile of v6, /device:TPU:1, one launch (start us, length us, event | category | flops | bytes accessed | tf_op | source)
XLA Modules:
  0.0 60.7 jit_solution(3717864392863365594)
XLA Ops:
  1.3 0.0 copy-start
  1.3 1.4 %copy-done = bf16[3,32,4,16,128]{4,3,2,1,0:T(8,128)(2,1)S(1)} copy-done((bf16[3,32,4,16,128]{4,3,2,1,0:T(8,128)(2,1)S(1)}, bf16[3,32,4,16,128]{4,3,2,1,0:T(8,128)(2,1)}, u32[]{:S(2)}) %copy-start) | copy-done | bytes 1572888
  2.7 0.0 copy-start.1
  2.7 0.0 copy-start.2
  2.7 0.2 shard_map.52
  2.9 0.8 %collective-permute-start.3 = (bf16[3,32,16,128]{3,2,1,0:T(8,128)(2,1)S(1)}, bf16[3,32,16,128]{3,2,1,0:T(8,128)(2,1)S(1)}, u32[]{:S(2)}, u32[]{:S(2)}) collective-permute-start(bf16[3,32,16,128]{3,2,1,0:T(8,128)(2,1)S(1)} %get-tuple-element.24), channel_id=1, source_target_pairs={{16,32},{48,64},{80,96},{112,128},{144,160},{176,192},{208,224},{2... | collective-permute-start | bytes 1179656 | tf_op jit(solution)/shard_map/ppermute | solution.py:419
  3.7 6.6 %collective-permute-start.2 = (bf16[3,32,16,128]{3,2,1,0:T(8,128)(2,1)S(1)}, bf16[3,32,16,128]{3,2,1,0:T(8,128)(2,1)S(1)}, u32[]{:S(2)}, u32[]{:S(2)}) collective-permute-start(bf16[3,32,16,128]{3,2,1,0:T(8,128)(2,1)S(1)} %get-tuple-element.23), channel_id=1, source_target_pairs={{0,16},{32,48},{64,80},{96,112},{128,144},{160,176},{192,208},{224... | collective-permute-start | bytes 1179656 | tf_op jit(solution)/shard_map/ppermute | solution.py:421
  10.3 0.6 shard_map.50
  10.9 3.2 %collective-permute-start = (bf16[128,128]{1,0:T(8,128)(2,1)S(1)}, bf16[128,128]{1,0:T(8,128)(2,1)S(1)}, u32[]{:S(2)}, u32[]{:S(2)}) collective-permute-start(bf16[128,128]{1,0:T(8,128)(2,1)S(1)} %get-tuple-element.18), channel_id=1, source_target_pairs={{0,1},{1,2},{2,3},{3,4},{4,5},{5,6},{6,7},{7,8},{8,9},{9,10},{10,1... | collective-permute-start | bytes 98312 | tf_op jit(solution)/shard_map/ppermute | solution.py:431
  14.1 0.0 collective-permute-start.1
  14.1 1.0 %collective-permute-done.low_ref = bf16[128,128]{1,0:T(8,128)(2,1)S(1)} collective-permute-done((bf16[128,128]{1,0:T(8,128)(2,1)S(1)}, bf16[128,128]{1,0:T(8,128)(2,1)S(1)}, u32[]{:S(2)}, u32[]{:S(2)}) %collective-permute-start) | collective-permute-done | bytes 32800 | tf_op jit(solution)/shard_map/ppermute | solution.py:431
  15.1 2.6 %collective-permute-done.1.high_ref = bf16[128,128]{1,0:T(8,128)(2,1)S(1)} collective-permute-done((bf16[128,128]{1,0:T(8,128)(2,1)S(1)}, bf16[128,128]{1,0:T(8,128)(2,1)S(1)}, u32[]{:S(2)}, u32[]{:S(2)}) %collective-permute-start.1) | collective-permute-done | bytes 32800 | tf_op jit(solution)/shard_map/ppermute | solution.py:432
  17.7 0.0 copy-done.1
  17.7 0.0 copy-done.2
  17.7 2.9 %shard_map.51 = (bf16[4,2,256,128]{3,2,1,0:T(8,128)(2,1)S(1)}, bf16[4,2,256,128]{3,2,1,0:T(8,128)(2,1)S(1)}, bf16[2,256,128]{2,1,0:T(8,128)(2,1)S(1)}, bf16[2,25...) custom-call(bf16[3,32,4,16,128]{4,3,2,1,0:T(8,128)(2,1)S(1)} %copy-done.1, ...), custom_call_target="tpu_custom_call" | custom-call | tf_op jit(solution)/shard_map/pallas_call | solution.py:436
  20.6 0.0 collective-permute-done.3.beside_ref
  20.6 0.9 %shard_map.53 = (bf16[4,256,128]{2,1,0:T(8,128)(2,1)S(1)}, bf16[4,256,128]{2,1,0:T(8,128)(2,1)S(1)}, f32[32,256]{1,0:T(8,128)S(1)}) custom-call(s32[1]{0:T(128)S(6)} %copy.7.flag_ref.refs_0_, bf16[3,32,4,16,128]{4,3,2,1,0:T(8,128)(2,1)S(1)} %copy-done.1, f32[3,4,16,128]{3,2,1,0:T(8,128)S(1)} %copy-done.2, ...), custom_call_target="tpu_custom_call" | custom-call | tf_op jit(solution)/shard_map/pallas_call | solution.py:449
  21.5 0.0 collective-permute-done.2.refs_6_
  21.6 1.3 %shard_map.54 = (bf16[4,256,128]{2,1,0:T(8,128)(2,1)S(1)}, bf16[4,256,128]{2,1,0:T(8,128)(2,1)S(1)}, f32[16,1,640]{2,1,0:T(1,128)S(1)}) custom-call(s32[1]{0:T(128)S(6)} %copy.7.flag_ref.refs_0_, bf16[3,32,4,16,128]{4,3,2,1,0:T(8,128)(2,1)S(1)} %copy-done.1, f32[3,4,16,128]{3,2,1,0:T(8,128)S(1)} %copy-done.2, ...), custom_call_target="tpu_custom_call" | custom-call | tf_op jit(solution)/shard_map/pallas_call | solution.py:457
  22.8 16.7 %all_to_all.10 = f32[16,1,640]{2,1,0:T(1,128)S(1)} all-to-all(f32[16,1,640]{2,1,0:T(1,128)S(1)} %get-tuple-element.27), channel_id=1, replica_groups=mesh['blk'=32,'gz'=16] {'gz'}, dimensions={0} | all-to-all | bytes 81920 | tf_op jit(solution)/shard_map/all_to_all | solution.py:466
  39.7 17.7 %all_to_all.11 = f32[32,1,640]{2,1,0:T(1,128)S(1)} all-to-all(f32[32,1,640]{2,1,0:T(1,128)S(1)} %broadcast_in_dim.2), channel_id=1, replica_groups=mesh['blk'=32,'gz'=16] {'blk'}, dimensions={0} | all-to-all | bytes 163840 | tf_op jit(solution)/shard_map/all_to_all | solution.py:468
  57.4 0.1 reduce_sum.21
  57.5 3.3 %shard_map.55 = (f32[4,16,4,16,128]{4,3,2,1,0:T(8,128)}, f32[32,32]{1,0:T(8,128)}) custom-call(f32[1,640]{1,0:T(1,128)S(1)} %reduce_sum.22.sum_ref, bf16[4,2,256,128]{3,2,1,0:T(8,128)(2,1)S(1)} %get-tuple-element.28.xhi_ref, bf16[4,2,256,128]{3,2,1,0:T(8,128)(2,1)S(1)} %get-tuple-element.29.xli_ref, bf16[4,256,128]{2,1,0:T(8,128)(2,1)S(1)} %get-tuple-element.30.xhn_ref, ...), custom_call_target="tpu_custom_call" | custom-call | tf_op jit(solution)/shard_map/pallas_call | solution.py:470
  (3 shorter events, 0.1 us)
Async XLA Ops:
  1.3 1.4 %copy-start = (bf16[3,32,4,16,128]{4,3,2,1,0:T(8,128)(2,1)S(1)}, bf16[3,32,4,16,128]{4,3,2,1,0:T(8,128)(2,1)}, u32[]{:S(2)}) copy-start(bf16[3,32,4,16,128]{4,3,2,1,0:T(8,128)(2,1)} %refs_1_.1) | copy-start | bytes 4718596
  2.7 15.1 %copy-start.1 = (bf16[3,32,4,16,128]{4,3,2,1,0:T(8,128)(2,1)S(1)}, bf16[3,32,4,16,128]{4,3,2,1,0:T(8,128)(2,1)}, u32[]{:S(2)}) copy-start(bf16[3,32,4,16,128]{4,3,2,1,0:T(8,128)(2,1)} %refs_1_.1) | copy-start | bytes 4718596
  2.7 15.1 %copy-start.2 = (f32[3,4,16,128]{3,2,1,0:T(8,128)S(1)}, f32[3,4,16,128]{3,2,1,0:T(8,128)}, u32[]{:S(2)}) copy-start(f32[3,4,16,128]{3,2,1,0:T(8,128)} %refs_2_.1) | copy-start | bytes 294916
  2.9 17.7 %collective-permute-start.3 = (bf16[3,32,16,128]{3,2,1,0:T(8,128)(2,1)S(1)}, bf16[3,32,16,128]{3,2,1,0:T(8,128)(2,1)S(1)}, u32[]{:S(2)}, u32[]{:S(2)}) collective-permute-start(bf16[3,32,16,128]{3,2,1,0:T(8,128)(2,1)S(1)} %get-tuple-element.24), channel_id=1, source_target_pairs={{16,32},{48,64},{80,96},{112,128},{144,160},{176,192},{208,224},{2... | collective-permute-start | bytes 1179656 | tf_op jit(solution)/shard_map/ppermute | solution.py:419
  3.7 17.9 %collective-permute-start.2 = (bf16[3,32,16,128]{3,2,1,0:T(8,128)(2,1)S(1)}, bf16[3,32,16,128]{3,2,1,0:T(8,128)(2,1)S(1)}, u32[]{:S(2)}, u32[]{:S(2)}) collective-permute-start(bf16[3,32,16,128]{3,2,1,0:T(8,128)(2,1)S(1)} %get-tuple-element.23), channel_id=1, source_target_pairs={{0,16},{32,48},{64,80},{96,112},{128,144},{160,176},{192,208},{224... | collective-permute-start | bytes 1179656 | tf_op jit(solution)/shard_map/ppermute | solution.py:421
  10.9 4.2 %collective-permute-start = (bf16[128,128]{1,0:T(8,128)(2,1)S(1)}, bf16[128,128]{1,0:T(8,128)(2,1)S(1)}, u32[]{:S(2)}, u32[]{:S(2)}) collective-permute-start(bf16[128,128]{1,0:T(8,128)(2,1)S(1)} %get-tuple-element.18), channel_id=1, source_target_pairs={{0,1},{1,2},{2,3},{3,4},{4,5},{5,6},{6,7},{7,8},{8,9},{9,10},{10,1... | collective-permute-start | bytes 98312 | tf_op jit(solution)/shard_map/ppermute | solution.py:431
  14.1 3.6 %collective-permute-start.1 = (bf16[128,128]{1,0:T(8,128)(2,1)S(1)}, bf16[128,128]{1,0:T(8,128)(2,1)S(1)}, u32[]{:S(2)}, u32[]{:S(2)}) collective-permute-start(bf16[128,128]{1,0:T(8,128)(2,1)S(1)} %get-tuple-element.19), channel_id=1, source_target_pairs={{1,0},{2,1},{3,2},{4,3},{5,4},{6,5},{7,6},{8,7},{9,8},{10,9},{11,1... | collective-permute-start | bytes 98312 | tf_op jit(solution)/shard_map/ppermute | solution.py:432
